TPU v7x, 128 devices: a whole 4x4x4 slice. The times are simulated.
128 devices in a mesh: blk: 8 (over y, z_hi), expert: 16 (over z_lo, x, core).
Axes of the slice: x: 4, y: 4, z: 4 (z_hi: 2, z_lo: 2; z = z_hi * 2 + z_lo), core: 2. Of those that a mesh axis runs over, the one named last changes fastest.
Arguments:
- query: bfloat16 [16, 1024, 4096], P('expert', 'blk'), may hold values from -16 to 16
- keys: bfloat16 [16, 1024, 256], P('expert', 'blk'), may hold values from -16 to 16
- values: bfloat16 [16, 1024, 256], P('expert', 'blk'), may hold values from -6 to 6
- grad_output: bfloat16 [16, 1024, 4096], P('expert', 'blk'), may hold values from -6 to 6
- expert_ids: int32 [16, 1024, 8], P('expert', 'blk'), may hold values from 0 to 127, all different within a row; in each aligned block of 128 rows (0 to 127, 128 to 255, ..., all dimensions but the last counted through in order) at most 9 rows name the same one
- gate_weights: float32 [16, 1024, 8], P('expert', 'blk'), may hold values from 0.05 to 0.5
- gate_up: bfloat16 [128, 4096, 1536], P(('blk', 'expert')), may hold values from -0.09375 to 0.09375
- down_weight: bfloat16 [128, 768, 4096], P(('blk', 'expert')), may hold values from -0.21875 to 0.21875
- saved_preact: bfloat16 [128, 128, 9, 1536], P(('blk', 'expert')), may hold values from -6 to 6
- block_order: int32 [16], replicated, may hold values from 0 to 15, each once
Outputs:
- query_gradient: bfloat16 [16, 1024, 4096], P('expert', 'blk')
- key_gradient: bfloat16 [16, 1024, 256], P('expert', 'blk')
- value_gradient: bfloat16 [16, 1024, 256], P('expert', 'blk')
Inputs may be any that keep to these rules, and one draw needn't show every extreme that they name: `expert_ids`: each token names 8 different experts; the 128 tokens of one device name one expert at most 9 times, and some device's tokens name some expert exactly 9 times.
All inputs are finite; a program needn't handle non-finite values.
Results may differ from a plain program's by a relative error of at most 0.019.
Values may be sent and summed in bfloat16 or wider, within the bound.
A program may use at most 192 MiB of HBM per device.

v0:
```python
import math

import jax
import jax.numpy as jnp
from jax import lax
from jax.sharding import PartitionSpec as P

HEAD_SIZE = 128


def passed_along(value, axis, steps):
    count = lax.axis_size(axis)
    pairs = [(source, (source + steps) % count) for source in range(count)]
    return lax.ppermute(value, axis, pairs)


def slot_numbers(flat_ids, expert_count):
    onehot = (flat_ids[:, None] == jnp.arange(expert_count, dtype=jnp.int32)[None, :]).astype(
        jnp.int32
    )
    before = jnp.cumsum(onehot, axis=0) - onehot
    return jnp.sum(before * onehot, axis=1)


def swiglu_grad(down_grad, saved):
    width = saved.shape[1] // 2
    gate = saved[:, :width]
    upper = saved[:, width:]
    sigma = jax.nn.sigmoid(gate)
    gate_grad = down_grad * upper * sigma * (1.0 + gate * (1.0 - sigma))
    upper_grad = down_grad * gate * sigma
    return jnp.concatenate([gate_grad, upper_grad], axis=1)


def positions_of(block_order, rows, half):
    return block_order[rows // half] * half + rows % half


def local(
    query,
    keys,
    values,
    grad_output,
    expert_ids,
    gate_weights,
    gate_up,
    down_weight,
    saved_preact,
    block_order,
):
    count_blk = lax.axis_size("blk")
    count_all = lax.axis_size(("blk", "expert"))
    blk_index = lax.axis_index("blk")
    rows_here = query.shape[1]
    width = grad_output.shape[2]
    most = saved_preact.shape[2]
    picks = expert_ids.shape[2]
    half = rows_here // 2
    kv_heads = keys.shape[2] // HEAD_SIZE
    group = query.shape[2] // keys.shape[2]
    scale = 1.0 / math.sqrt(HEAD_SIZE)
    grad_rows = grad_output[0]
    flat_ids = expert_ids[0].reshape(-1)
    slots = slot_numbers(flat_ids, count_all)
    target = flat_ids * most + slots
    token_of = jnp.arange(rows_here * picks, dtype=jnp.int32) // picks
    outgoing = (
        jnp.zeros((count_all * most, width), jnp.bfloat16).at[target].set(grad_rows[token_of])
    )
    outgoing = outgoing.reshape(count_all, most, width)
    incoming = lax.all_to_all(outgoing, ("blk", "expert"), split_axis=0, concat_axis=0, tiled=True)
    flat_rows = incoming.reshape(count_all * most, width)
    down_grad = lax.dot_general(
        flat_rows, down_weight[0], (((1,), (1,)), ((), ())), preferred_element_type=jnp.float32
    )
    saved = saved_preact[0].reshape(count_all * most, -1).astype(jnp.float32)
    act_grad = swiglu_grad(down_grad, saved).astype(jnp.bfloat16)
    expert_back = lax.dot_general(
        act_grad, gate_up[0], (((1,), (1,)), ((), ())), preferred_element_type=jnp.float32
    ).astype(jnp.bfloat16)
    expert_back = expert_back.reshape(count_all, most, width)
    returned = lax.all_to_all(
        expert_back, ("blk", "expert"), split_axis=0, concat_axis=0, tiled=True
    )
    picked = returned.reshape(count_all * most, width)[target].astype(jnp.float32)
    weighted = jnp.sum(
        (picked * gate_weights[0].reshape(-1, 1)).reshape(rows_here, picks, width), axis=1
    )
    residual_grad = (grad_rows.astype(jnp.float32) + weighted).astype(jnp.bfloat16)
    query_four = query[0].reshape(rows_here, kv_heads, group, HEAD_SIZE)
    gradient_four = residual_grad.reshape(rows_here, kv_heads, group, HEAD_SIZE)
    local_rows = jnp.arange(rows_here, dtype=jnp.int32)
    own_pos = positions_of(block_order, blk_index * rows_here + local_rows, half)
    row_max = jnp.full((kv_heads, group, rows_here), -1e30, jnp.float32)
    key_piece = lax.all_gather(keys[0], "blk", axis=0, tiled=True)
    value_piece = lax.all_gather(values[0], "blk", axis=0, tiled=True)
    count = key_piece.shape[0]
    key_pos = positions_of(block_order, jnp.arange(count, dtype=jnp.int32), half)
    keys_three = key_piece.reshape(count, kv_heads, HEAD_SIZE)
    values_three = value_piece.reshape(count, kv_heads, HEAD_SIZE)
    scores = (
        jnp.einsum("tgjd,rgd->gjtr", query_four, keys_three, preferred_element_type=jnp.float32)
        * scale
    )
    visible = own_pos[:, None] >= key_pos[None, :]
    new_max = jnp.maximum(row_max, jnp.max(jnp.where(visible, scores, -1e30), axis=-1))
    weights = jnp.where(visible, jnp.exp(scores - new_max[..., None]), 0.0)
    accum = jnp.einsum(
        "gjtr,rgd->gjtd",
        weights.astype(jnp.bfloat16),
        values_three,
        preferred_element_type=jnp.float32,
    )
    row_max, total, accum = (new_max, jnp.sum(weights, axis=-1), accum)
    attn_out = accum / total[..., None]
    log_total = row_max + jnp.log(total)
    delta = jnp.sum(
        jnp.transpose(gradient_four.astype(jnp.float32), (1, 2, 0, 3)) * attn_out, axis=-1
    )

    def grads_for(lower, upper, block, key_pos):
        count = upper - lower
        keys_three = block[0].reshape(-1, count, HEAD_SIZE)
        values_three = block[1].reshape(-1, count, HEAD_SIZE)
        key_rows = keys_three.shape[0]
        scores = (
            jnp.einsum("tgjd,rgd->gjtr", query_four, keys_three, preferred_element_type=jnp.float32)
            * scale
        )
        visible = own_pos[:, None] >= key_pos[None, :]
        probs = jnp.where(visible, jnp.exp(scores - log_total[..., None]), 0.0)
        value_part = jnp.einsum(
            "gjtr,tgjd->rgd",
            probs.astype(jnp.bfloat16),
            gradient_four,
            preferred_element_type=jnp.float32,
        )
        prob_grad = jnp.einsum(
            "tgjd,rgd->gjtr", gradient_four, values_three, preferred_element_type=jnp.float32
        )
        score_grad = (probs * (prob_grad - delta[..., None])).astype(jnp.bfloat16)
        query_term = (
            jnp.einsum("gjtr,rgd->tgjd", score_grad, keys_three, preferred_element_type=jnp.float32)
            * scale
        )
        key_part = (
            jnp.einsum("gjtr,tgjd->rgd", score_grad, query_four, preferred_element_type=jnp.float32)
            * scale
        )
        pair_part = jnp.stack(
            [
                key_part.reshape(key_rows, count * HEAD_SIZE),
                value_part.reshape(key_rows, count * HEAD_SIZE),
            ]
        )
        return (query_term, pair_part)

    def source_pos(source):
        return positions_of(block_order, source * rows_here + local_rows, half)

    query_start = jnp.zeros((rows_here, kv_heads, group, HEAD_SIZE), jnp.float32)

    def pass_step(step, carry):
        block, pair_acc, query_acc = carry
        source = (blk_index - step) % count_blk
        query_term, pair_part = grads_for(0, kv_heads, block, source_pos(source))
        block = passed_along(block, "blk", 1)
        pair_acc = passed_along((pair_acc + pair_part).astype(jnp.bfloat16), "blk", 1).astype(
            jnp.float32
        )
        return (block, pair_acc, query_acc + query_term)

    block_start = jnp.stack([keys[0], values[0]])
    final = lax.fori_loop(
        0,
        count_blk,
        pass_step,
        (block_start, jnp.zeros(block_start.shape, jnp.float32), query_start),
    )
    pair_grad = final[1]
    query_acc = final[2]
    query_gradient = query_acc.reshape(1, rows_here, -1).astype(jnp.bfloat16)
    key_gradient = pair_grad[0][None].astype(jnp.bfloat16)
    value_gradient = pair_grad[1][None].astype(jnp.bfloat16)
    return (query_gradient, key_gradient, value_gradient)


def solution(mesh):
    in_specs = (
        P("expert", "blk", None),
        P("expert", "blk", None),
        P("expert", "blk", None),
        P("expert", "blk", None),
        P("expert", "blk", None),
        P("expert", "blk", None),
        P(("blk", "expert"), None, None),
        P(("blk", "expert"), None, None),
        P(("blk", "expert"), None, None, None),
        P(),
    )
    out_specs = (P("expert", "blk", None), P("expert", "blk", None), P("expert", "blk", None))
    return jax.shard_map(local, mesh=mesh, in_specs=in_specs, out_specs=out_specs, check_vma=False)
```

profile of v0, /device:TPU:36, one launch (start us, length us, event | category | flops | bytes accessed | tf_op | source)
XLA Modules:
  0.0 943.1 jit_solution(7586381007304720622)
XLA Ops:
  3.5 7.7 gather_fusion
  11.2 18.4 %scatter_custom_fusion = bf16[1152,4096]{1,0:T(8,128)(2,1)} fusion(s32[1024]{0:T(1024)S(1)} %bitcast.414, bf16[1024,4096]{1,0:T(8,128)(2,1)} %gather_fusion, bf16[]{:T(256)} %constant.237.clone.1), kind=kCustom, calls=%fused_computation.62 | custom fusion | bytes 9437696 | tf_op jit(solution)/shard_map/scatter | solution.py:68
  29.7 15.1 %reshape.388 = bf16[128,9,4096]{2,1,0:T(8,128)(2,1)} reshape(bf16[1152,4096]{1,0:T(8,128)(2,1)} %scatter_custom_fusion) | data formatting | bytes 18874368 | tf_op jit(solution)/shard_map/reshape | solution.py:70
  44.8 10.7 %all-to-all-start = ((bf16[128,9,4096]{2,1,0:T(8,128)(2,1)}), bf16[128,9,4096]{2,1,0:T(8,128)(2,1)}, u32[]{:S(2)}, u32[]{:S(2)}) async-start(bf16[128,9,4096]{2,1,0:T(8,128)(2,1)} %reshape.388), calls=%async_computation | async-start | bytes 33554432 | tf_op jit(solution)/shard_map/all_to_all | solution.py:71
  55.5 9.1 copy.75
  64.6 9.8 %reshape.394 = f32[1152,1536]{1,0:T(8,128)} reshape(f32[1,128,9,1536]{3,2,1,0:T(8,128)} %copy.75) | data formatting | bytes 14155776 | tf_op jit(solution)/shard_map/convert_element_type | solution.py:76
  74.3 6.5 fusion.52
  80.8 5.2 copy.106
  86.0 5.2 copy.107
  91.1 192.4 %all-to-all-done = bf16[128,9,4096]{2,1,0:T(8,128)(2,1)} async-done(((bf16[128,9,4096]{2,1,0:T(8,128)(2,1)}), bf16[128,9,4096]{2,1,0:T(8,128)(2,1)}, u32[]{:S(2)}, u32[]{:S(2)}) %all-to-all-start) | async-done | bytes 9437216 | tf_op jit(solution)/shard_map/all_to_all | solution.py:71
  283.5 15.8 %reshape.389 = bf16[1152,4096]{1,0:T(8,128)(2,1)} reshape(bf16[128,9,4096]{2,1,0:T(8,128)(2,1)} %all-to-all-done) | data formatting | bytes 18874368 | tf_op jit(solution)/shard_map/reshape | solution.py:72
  299.3 16.3 %multiply_convert_fusion.1 = (bf16[1152,768]{0,1:T(8,128)(2,1)S(1)}, bf16[1152,768]{0,1:T(8,128)(2,1)}) fusion(f32[1152,768]{0,1:T(8,128)} %copy.107, f32[1152,768]{0,1:T(8,128)} %copy.106, bf16[1152,4096]{1,0:T(8,128)(2,1)} %reshape.389, bf16[1,768,4096]{2,1,0:T(8,128)(2,1)} %param.19), kind=kOutput, calls=%fused_computation.68 | convolution fusion | flops 7259258880 | bytes 26345472 | tf_op jit(solution)/shard_map/dot_general | solution.py:73
  315.6 21.0 %convolution_convert_fusion = bf16[1152,4096]{1,0:T(8,128)(2,1)} fusion(bf16[1,4096,1536]{2,1,0:T(8,128)(2,1)} %param.18, bf16[1152,768]{0,1:T(8,128)(2,1)} %get-tuple-element.413, bf16[1152,768]{0,1:T(8,128)(2,1)S(1)} %get-tuple-element.412), kind=kOutput, calls=%fused_computation.54 | convolution fusion | flops 14507311104 | bytes 25559040 | tf_op jit(solution)/shard_map/dot_general | solution.py:78
  336.6 15.1 %reshape.390 = bf16[128,9,4096]{2,1,0:T(8,128)(2,1)} reshape(bf16[1152,4096]{1,0:T(8,128)(2,1)} %convolution_convert_fusion) | data formatting | bytes 18874368 | tf_op jit(solution)/shard_map/reshape | solution.py:81
  351.7 22.9 %all-to-all-start.1 = ((bf16[128,9,4096]{2,1,0:T(8,128)(2,1)}), bf16[128,9,4096]{2,1,0:T(8,128)(2,1)}, u32[]{:S(2)}, u32[]{:S(2)}) async-start(bf16[128,9,4096]{2,1,0:T(8,128)(2,1)} %reshape.390), calls=%async_computation.1 | async-start | bytes 33554432 | tf_op jit(solution)/shard_map/all_to_all | solution.py:82
  376.7 247.5 %all-gather.1 = bf16[1,1024,256]{2,1,0:T(8,128)(2,1)S(1)} all-gather(bf16[1,128,256]{2,1,0:T(8,128)(2,1)S(1)} %copy-done.4), channel_id=3, replica_groups=mesh['blk'=8,'expert'=16] {'blk'}, dimensions={1}, use_global_device_ids=true | all-gather | bytes 589824 | tf_op jit(solution)/shard_map/all_gather | solution.py:96
  626.9 9.8 %fusion.43 = s32[128]{0:T(128)S(1)} fusion(s32[]{:T(128)} %bitcast.18, s32[]{:T(128)} %bitcast.19, s32[]{:T(128)} %bitcast.20, s32[]{:T(128)} %bitcast.21, s32[]{:T(128)} %bitcast.22, s32[]{:T(128)} %bitcast.24, s32[]{:T(128)} %bitcast.23, s32[]{:T(128)} %bitcast.1, s32[]{:T(128)} %bitcast.3, s32[]{:T(128)} %bitcast.5, s32[]{:T(128)} %bitcast.7, ...), kind=kLoop, calls=%fused_computation.145 | loop fusion | flops 8064 | bytes 580 | tf_op jit(solution)/shard_map/add | solution.py:36
  636.7 4.1 compare_select_fusion.15
  640.8 5.6 fusion.39
  646.7 31.2 %all-gather = bf16[1,1024,256]{1,2,0:T(8,128)(2,1)S(1)} all-gather(bf16[1,128,256]{1,2,0:T(8,128)(2,1)S(1)} %copy.63), channel_id=2, replica_groups=mesh['blk'=8,'expert'=16] {'blk'}, dimensions={1}, use_global_device_ids=true | all-gather | bytes 589824 | tf_op jit(solution)/shard_map/all_gather | solution.py:95
  677.9 7.2 fusion.15
  685.2 9.1 fusion.19
  694.3 15.8 %reshape.391 = bf16[1152,4096]{1,0:T(8,128)(2,1)} reshape(bf16[128,9,4096]{2,1,0:T(8,128)(2,1)} %all-to-all-done.1) | data formatting | bytes 18874368 | tf_op jit(solution)/shard_map/reshape | solution.py:85
  710.1 20.1 %gather_fusion.1 = bf16[1024,4096]{1,0:T(8,128)(2,1)} fusion(bf16[1152,4096]{1,0:T(8,128)(2,1)} %reshape.391, s32[1024]{0:T(1024)S(1)} %broadcast_clamp_fusion), kind=kCustom, calls=%fused_computation.1 | custom fusion | bytes 16781312 | tf_op jit(solution)/shard_map/gather | solution.py:85
  730.3 13.2 %fusion.14 = f32[128,4096]{1,0:T(8,128)} fusion(bf16[1024,4096]{1,0:T(8,128)(2,1)} %gather_fusion.1, f32[128,8]{1,0:T(8,128)S(1)} %copy.78), kind=kLoop, calls=%fused_computation.48 | loop fusion | flops 12058624 | bytes 10489856 | tf_op jit(solution)/shard_map/reduce_sum | solution.py:86
  749.1 9.3 fusion.31
  758.3 179.8 %while.21 = (s32[]{:T(128)}, bf16[2,128,256]{1,2,0:T(8,128)(2,1)S(1)}, f32[2,128,256]{1,2,0:T(8,128)S(1)}, f32[128,2,16,128]{3,0,2,1:T(8,128)}, s32[128]{0:T(128...) while((s32[]{:T(128)}, ...), condition=%wide.region_9.10_spmd.clone, body=%wide.region_8.9_spmd.clone.sunk | while | flops 676716288 | bytes 20973624 | solution.py:174
  759.5 10.2 %fusion.98 = s32[128]{0:T(128)S(1)} fusion(s32[]{:T(128)} %bitcast.381, s32[]{:T(128)} %bitcast.382, s32[]{:T(128)} %bitcast.383, s32[]{:T(128)} %bitcast.384, s32[]{:T(128)} %bitcast.385, s32[]{:T(128)} %bitcast.386, s32[]{:T(128)} %bitcast.387, s32[]{:T(128)} %bitcast.388, s32[]{:T(128)} %bitcast.389, s32[]{:T(128)} %bitcast.390, s32[]{:T(128)} %bitcast.391, ...), kind=kLoop, calls=%fused_computation.41.clone.1 | loop fusion | flops 7936 | bytes 580 | tf_op jit(solution)/shard_map/while/body/eval_jaxpr/add | solution.py:36
  771.8 4.0 collective-permute-start.1
  777.7 3.4 collective-permute-done.1
  783.2 10.2 %fusion.98 = s32[128]{0:T(128)S(1)} fusion(s32[]{:T(128)} %bitcast.381, s32[]{:T(128)} %bitcast.382, s32[]{:T(128)} %bitcast.383, s32[]{:T(128)} %bitcast.384, s32[]{:T(128)} %bitcast.385, s32[]{:T(128)} %bitcast.386, s32[]{:T(128)} %bitcast.387, s32[]{:T(128)} %bitcast.388, s32[]{:T(128)} %bitcast.389, s32[]{:T(128)} %bitcast.390, s32[]{:T(128)} %bitcast.391, ...), kind=kLoop, calls=%fused_computation.41.clone.1 | loop fusion | flops 7936 | bytes 580 | tf_op jit(solution)/shard_map/while/body/eval_jaxpr/add | solution.py:36
  796.6 3.5 bitcast_add_fusion.2
  800.0 4.2 collective-permute-done.1
  805.1 10.2 %fusion.98 = s32[128]{0:T(128)S(1)} fusion(s32[]{:T(128)} %bitcast.381, s32[]{:T(128)} %bitcast.382, s32[]{:T(128)} %bitcast.383, s32[]{:T(128)} %bitcast.384, s32[]{:T(128)} %bitcast.385, s32[]{:T(128)} %bitcast.386, s32[]{:T(128)} %bitcast.387, s32[]{:T(128)} %bitcast.388, s32[]{:T(128)} %bitcast.389, s32[]{:T(128)} %bitcast.390, s32[]{:T(128)} %bitcast.391, ...), kind=kLoop, calls=%fused_computation.41.clone.1 | loop fusion | flops 7936 | bytes 580 | tf_op jit(solution)/shard_map/while/body/eval_jaxpr/add | solution.py:36
  820.4 3.5 bitcast_add_fusion.2
  827.7 10.2 %fusion.98 = s32[128]{0:T(128)S(1)} fusion(s32[]{:T(128)} %bitcast.381, s32[]{:T(128)} %bitcast.382, s32[]{:T(128)} %bitcast.383, s32[]{:T(128)} %bitcast.384, s32[]{:T(128)} %bitcast.385, s32[]{:T(128)} %bitcast.386, s32[]{:T(128)} %bitcast.387, s32[]{:T(128)} %bitcast.388, s32[]{:T(128)} %bitcast.389, s32[]{:T(128)} %bitcast.390, s32[]{:T(128)} %bitcast.391, ...), kind=kLoop, calls=%fused_computation.41.clone.1 | loop fusion | flops 7936 | bytes 580 | tf_op jit(solution)/shard_map/while/body/eval_jaxpr/add | solution.py:36
  841.1 3.5 bitcast_add_fusion.2
  844.5 4.2 collective-permute-done.1
  849.6 10.2 %fusion.98 = s32[128]{0:T(128)S(1)} fusion(s32[]{:T(128)} %bitcast.381, s32[]{:T(128)} %bitcast.382, s32[]{:T(128)} %bitcast.383, s32[]{:T(128)} %bitcast.384, s32[]{:T(128)} %bitcast.385, s32[]{:T(128)} %bitcast.386, s32[]{:T(128)} %bitcast.387, s32[]{:T(128)} %bitcast.388, s32[]{:T(128)} %bitcast.389, s32[]{:T(128)} %bitcast.390, s32[]{:T(128)} %bitcast.391, ...), kind=kLoop, calls=%fused_computation.41.clone.1 | loop fusion | flops 7936 | bytes 580 | tf_op jit(solution)/shard_map/while/body/eval_jaxpr/add | solution.py:36
  864.7 3.5 bitcast_add_fusion.2
  872.1 10.2 %fusion.98 = s32[128]{0:T(128)S(1)} fusion(s32[]{:T(128)} %bitcast.381, s32[]{:T(128)} %bitcast.382, s32[]{:T(128)} %bitcast.383, s32[]{:T(128)} %bitcast.384, s32[]{:T(128)} %bitcast.385, s32[]{:T(128)} %bitcast.386, s32[]{:T(128)} %bitcast.387, s32[]{:T(128)} %bitcast.388, s32[]{:T(128)} %bitcast.389, s32[]{:T(128)} %bitcast.390, s32[]{:T(128)} %bitcast.391, ...), kind=kLoop, calls=%fused_computation.41.clone.1 | loop fusion | flops 7936 | bytes 580 | tf_op jit(solution)/shard_map/while/body/eval_jaxpr/add | solution.py:36
  886.1 3.5 bitcast_add_fusion.2
  889.5 3.6 collective-permute-done.1
  894.0 10.2 %fusion.98 = s32[128]{0:T(128)S(1)} fusion(s32[]{:T(128)} %bitcast.381, s32[]{:T(128)} %bitcast.382, s32[]{:T(128)} %bitcast.383, s32[]{:T(128)} %bitcast.384, s32[]{:T(128)} %bitcast.385, s32[]{:T(128)} %bitcast.386, s32[]{:T(128)} %bitcast.387, s32[]{:T(128)} %bitcast.388, s32[]{:T(128)} %bitcast.389, s32[]{:T(128)} %bitcast.390, s32[]{:T(128)} %bitcast.391, ...), kind=kLoop, calls=%fused_computation.41.clone.1 | loop fusion | flops 7936 | bytes 580 | tf_op jit(solution)/shard_map/while/body/eval_jaxpr/add | solution.py:36
  906.4 3.4 collective-permute-start.1
  909.7 3.5 bitcast_add_fusion.2
  917.1 10.2 %fusion.98 = s32[128]{0:T(128)S(1)} fusion(s32[]{:T(128)} %bitcast.381, s32[]{:T(128)} %bitcast.382, s32[]{:T(128)} %bitcast.383, s32[]{:T(128)} %bitcast.384, s32[]{:T(128)} %bitcast.385, s32[]{:T(128)} %bitcast.386, s32[]{:T(128)} %bitcast.387, s32[]{:T(128)} %bitcast.388, s32[]{:T(128)} %bitcast.389, s32[]{:T(128)} %bitcast.390, s32[]{:T(128)} %bitcast.391, ...), kind=kLoop, calls=%fused_computation.41.clone.1 | loop fusion | flops 7936 | bytes 580 | tf_op jit(solution)/shard_map/while/body/eval_jaxpr/add | solution.py:36
  932.3 3.5 bitcast_add_fusion.2
  (169 shorter events, 67.8 us)
Async XLA Ops:
  0.6 2.9 copy-start
  44.8 238.7 %all-to-all-start = ((bf16[128,9,4096]{2,1,0:T(8,128)(2,1)}), bf16[128,9,4096]{2,1,0:T(8,128)(2,1)}, u32[]{:S(2)}, u32[]{:S(2)}) async-start(bf16[128,9,4096]{2,1,0:T(8,128)(2,1)} %reshape.388), calls=%async_computation | async-start | bytes 33554432 | tf_op jit(solution)/shard_map/all_to_all | solution.py:71
  351.7 24.6 %copy-start.5 = (bf16[1,128,256]{2,1,0:T(8,128)(2,1)S(1)}, bf16[1,128,256]{2,1,0:T(8,128)(2,1)}, u32[]{:S(2)}) copy-start(bf16[1,128,256]{2,1,0:T(8,128)(2,1)} %param.13) | copy-start | bytes 196612
  351.7 24.7 %copy-start.6 = (f32[1,128,8]{1,2,0:T(8,128)S(1)}, f32[1,128,8]{1,2,0:T(8,128)}, u32[]{:S(2)}) copy-start(f32[1,128,8]{1,2,0:T(8,128)} %param.17) | copy-start | bytes 12292
  351.7 24.8 %copy-start.4 = (bf16[1,128,256]{2,1,0:T(8,128)(2,1)S(1)}, bf16[1,128,256]{2,1,0:T(8,128)(2,1)}, u32[]{:S(2)}) copy-start(bf16[1,128,256]{2,1,0:T(8,128)(2,1)} %param.14) | copy-start | bytes 196612
  351.7 342.6 %all-to-all-start.1 = ((bf16[128,9,4096]{2,1,0:T(8,128)(2,1)}), bf16[128,9,4096]{2,1,0:T(8,128)(2,1)}, u32[]{:S(2)}, u32[]{:S(2)}) async-start(bf16[128,9,4096]{2,1,0:T(8,128)(2,1)} %reshape.390), calls=%async_computation.1 | async-start | bytes 33554432 | tf_op jit(solution)/shard_map/all_to_all | solution.py:82
  374.6 250.6 %copy-start.2 = (bf16[1,128,4096]{2,1,0:T(8,128)(2,1)S(1)}, bf16[1,128,4096]{2,1,0:T(8,128)(2,1)}, u32[]{:S(2)}) copy-start(bf16[1,128,4096]{2,1,0:T(8,128)(2,1)} %param.12) | copy-start | bytes 3145732
  374.6 251.6 %copy-start.1 = (s32[16]{0:T(128)S(1)}, s32[16]{0:T(128)}, u32[]{:S(2)}) copy-start(s32[16]{0:T(128)} %param.21) | copy-start | bytes 196
  746.4 2.6 copy-start.3
  758.6 22.5 %collective-permute-start = (bf16[2,128,256]{1,2,0:T(8,128)(2,1)S(1)}, bf16[2,128,256]{1,2,0:T(8,128)(2,1)S(1)}, u32[]{:S(2)}, u32[]{:S(2)}) collective-permute-start(bf16[2,128,256]{1,2,0:T(8,128)(2,1)S(1)} %copy.113), channel_id=1, source_target_pairs={{0,16},{16,32},{32,48},{48,64},{64,80},{80,96},{96,112},{112,0},{1... | collective-permute-start | bytes 393224 | tf_op jit(solution)/shard_map/while/body/eval_jaxpr/ppermute | solution.py:14
  771.8 9.3 collective-permute-start.1
  781.2 23.1 %collective-permute-start = (bf16[2,128,256]{1,2,0:T(8,128)(2,1)S(1)}, bf16[2,128,256]{1,2,0:T(8,128)(2,1)S(1)}, u32[]{:S(2)}, u32[]{:S(2)}) collective-permute-start(bf16[2,128,256]{1,2,0:T(8,128)(2,1)S(1)} %copy.113), channel_id=1, source_target_pairs={{0,16},{16,32},{32,48},{48,64},{64,80},{80,96},{96,112},{112,0},{1... | collective-permute-start | bytes 393224 | tf_op jit(solution)/shard_map/while/body/eval_jaxpr/ppermute | solution.py:14
  795.6 8.7 collective-permute-start.1
  804.3 21.9 %collective-permute-start = (bf16[2,128,256]{1,2,0:T(8,128)(2,1)S(1)}, bf16[2,128,256]{1,2,0:T(8,128)(2,1)S(1)}, u32[]{:S(2)}, u32[]{:S(2)}) collective-permute-start(bf16[2,128,256]{1,2,0:T(8,128)(2,1)S(1)} %copy.113), channel_id=1, source_target_pairs={{0,16},{16,32},{32,48},{48,64},{64,80},{80,96},{96,112},{112,0},{1... | collective-permute-start | bytes 393224 | tf_op jit(solution)/shard_map/while/body/eval_jaxpr/ppermute | solution.py:14
  817.5 8.7 collective-permute-start.1
  826.2 22.5 %collective-permute-start = (bf16[2,128,256]{1,2,0:T(8,128)(2,1)S(1)}, bf16[2,128,256]{1,2,0:T(8,128)(2,1)S(1)}, u32[]{:S(2)}, u32[]{:S(2)}) collective-permute-start(bf16[2,128,256]{1,2,0:T(8,128)(2,1)S(1)} %copy.113), channel_id=1, source_target_pairs={{0,16},{16,32},{32,48},{48,64},{64,80},{80,96},{96,112},{112,0},{1... | collective-permute-start | bytes 393224 | tf_op jit(solution)/shard_map/while/body/eval_jaxpr/ppermute | solution.py:14
  840.1 8.7 collective-permute-start.1
  848.8 21.9 %collective-permute-start = (bf16[2,128,256]{1,2,0:T(8,128)(2,1)S(1)}, bf16[2,128,256]{1,2,0:T(8,128)(2,1)S(1)}, u32[]{:S(2)}, u32[]{:S(2)}) collective-permute-start(bf16[2,128,256]{1,2,0:T(8,128)(2,1)S(1)} %copy.113), channel_id=1, source_target_pairs={{0,16},{16,32},{32,48},{48,64},{64,80},{80,96},{96,112},{112,0},{1... | collective-permute-start | bytes 393224 | tf_op jit(solution)/shard_map/while/body/eval_jaxpr/ppermute | solution.py:14
  862.0 8.7 collective-permute-start.1
  870.7 22.4 %collective-permute-start = (bf16[2,128,256]{1,2,0:T(8,128)(2,1)S(1)}, bf16[2,128,256]{1,2,0:T(8,128)(2,1)S(1)}, u32[]{:S(2)}, u32[]{:S(2)}) collective-permute-start(bf16[2,128,256]{1,2,0:T(8,128)(2,1)S(1)} %copy.113), channel_id=1, source_target_pairs={{0,16},{16,32},{32,48},{48,64},{64,80},{80,96},{96,112},{112,0},{1... | collective-permute-start | bytes 393224 | tf_op jit(solution)/shard_map/while/body/eval_jaxpr/ppermute | solution.py:14
  884.5 8.7 collective-permute-start.1
  893.2 21.9 %collective-permute-start = (bf16[2,128,256]{1,2,0:T(8,128)(2,1)S(1)}, bf16[2,128,256]{1,2,0:T(8,128)(2,1)S(1)}, u32[]{:S(2)}, u32[]{:S(2)}) collective-permute-start(bf16[2,128,256]{1,2,0:T(8,128)(2,1)S(1)} %copy.113), channel_id=1, source_target_pairs={{0,16},{16,32},{32,48},{48,64},{64,80},{80,96},{96,112},{112,0},{1... | collective-permute-start | bytes 393224 | tf_op jit(solution)/shard_map/while/body/eval_jaxpr/ppermute | solution.py:14
  906.4 8.7 collective-permute-start.1
  915.1 23.0 %collective-permute-start = (bf16[2,128,256]{1,2,0:T(8,128)(2,1)S(1)}, bf16[2,128,256]{1,2,0:T(8,128)(2,1)S(1)}, u32[]{:S(2)}, u32[]{:S(2)}) collective-permute-start(bf16[2,128,256]{1,2,0:T(8,128)(2,1)S(1)} %copy.113), channel_id=1, source_target_pairs={{0,16},{16,32},{32,48},{48,64},{64,80},{80,96},{96,112},{112,0},{1... | collective-permute-start | bytes 393224 | tf_op jit(solution)/shard_map/while/body/eval_jaxpr/ppermute | solution.py:14
  929.5 8.7 collective-permute-start.1
where the time goes:
time: 955 us; the launch traced here: 943 us
  blocking collectives  279 us (29%)
  waiting for transfers between devices  217 us (23%)
  local copies, waits for them, and re-layouts  161 us (17%)
  other arithmetic  131 us (14%)
  matrix products  95.7 us (10%)
  starting transfers between devices  57.2 us (6%)
    all_gather x1, blocking collectives, local(): value_piece = lax.all_gather(values[0], 'blk', axis=0, tiled=True)  248 us
    all_to_all x1, waiting for transfers between devices, local(): lax.all_to_all(outgoing, ('blk', 'expert'), split_axis=0, concat_axis=0,...  192 us
    add x10, other arithmetic, positions_of(): return block_order[rows // half] * half + rows % half  97.2 us
    all_gather x1, blocking collectives, local(): key_piece = lax.all_gather(keys[0], 'blk', axis=0, tiled=True)  31.2 us
    dot_general x8, matrix products, grads_for(): jnp.einsum('gjtr,rgd->tgjd', score_grad, keys_three, preferred_element_ty...  26.1 us
    ppermute x16, waiting for transfers between devices, passed_along(): return lax.ppermute(value, axis, pairs)  24.3 us
    ppermute x16, starting transfers between devices, passed_along(): return lax.ppermute(value, axis, pairs)  23.7 us
    all_to_all x1, starting transfers between devices, local(): lax.all_to_all(expert_back, ('blk', 'expert'), split_axis=0, concat_axis=...  22.9 us
  transfers between devices with their start and end apart: 18, of which 9 were waited for; matrix products, arithmetic and copies ran while one was open for 22% of the time, Pallas kernels for 0%

commit v1 on v0

v1 whole, which is shorter than its diff:
```python
import math

import jax
import jax.numpy as jnp
from jax import lax
from jax.experimental import pallas as pl
from jax.experimental.pallas import tpu as pltpu
from jax.sharding import PartitionSpec as P

MESH = pl.DeviceIdType.MESH
HEAD = 128
ORDERS = ((0, 1, 2), (1, 2, 0), (2, 0, 1))
BF = jnp.bfloat16
F32 = jnp.float32


def coords():
    b = lax.axis_index("blk")
    e = lax.axis_index("expert")
    return (e // 2) % 4, b // 2, (b % 2) * 2 + e // 8, e % 2


def device_of(x, y, z, c):
    return (y * 2 + z // 2, ((z % 2) * 4 + x) * 2 + c)


def exchange_kernel(
    tok, ret, wts,
    g_ref, k_ref, v_ref, saved_ref, down_ref, gate_ref,
    res_ref, kf_ref, vf_ref,
    S, A, B, R, X, act, D, G, sv,
    ssem, rsem, lsem, kvs, kvr, dsem, gsem, svsem,
):
    x, y, z, c = coords()
    cc = (x, y, z)
    bme = lax.axis_index("blk")
    eme = lax.axis_index("expert")

    def dv(dim, v, core):
        t = [x, y, z]
        t[dim] = v
        return device_of(t[0], t[1], t[2], core)

    barrier = pltpu.get_barrier_semaphore()
    peers = [dv(dim, (cc[dim] + k) & 3, c ^ dc) for dim in range(3) for k in range(1, 4) for dc in range(2)]
    peers.append(dv(0, x, c ^ 1))
    peers += [device_of(x, (y + k) & 3, z ^ 2, c) for k in range(1, 4)]
    for p in peers:
        pl.semaphore_signal(barrier, inc=1, device_id=p, device_id_type=MESH)

    pltpu.make_async_copy(down_ref, D, dsem).start()

    def gate_copy(block, slot):
        return pltpu.make_async_copy(gate_ref.at[pl.ds(block * 512, 512)], G.at[slot], gsem.at[slot])

    def saved_copy(j):
        return pltpu.make_async_copy(saved_ref.at[pl.ds(3 * j, 3)], sv, svsem)

    gate_copy(0, 0).start()
    gate_copy(1, 1).start()
    saved_copy(0).start()

    def build(j):
        def body(i, carry):
            for u in range(8):
                row = j * 384 + i * 8 + u
                S[j * 12 + i // 4, i % 4, u] = g_ref[tok[row]]
            return carry

        lax.fori_loop(0, 48, body, 0)

    build(0)
    pl.semaphore_wait(barrier, len(peers))

    def remote(src, dst, ph, j, q, dev):
        return pltpu.make_async_remote_copy(
            src, dst, ssem.at[ph, j, q], rsem.at[ph, j, q], device_id=dev, device_id_type=MESH
        )

    def phase(ph, j):
        for k in (2, 1, 3, 0):
            for q, (a, b, d) in enumerate(ORDERS):
                ma, mb, md = cc[a], cc[b], cc[d]
                n = 3 * j + q
                if ph in (0, 5):
                    v = (ma + k) & 3
                    if ph == 0:
                        ops = [(S.at[n * 4 + v], A.at[n, ma], dv(a, v, c), k == 0)]
                    else:
                        ops = [(A.at[n, v], S.at[n * 4 + ma], dv(a, v, c), k == 0)]
                elif ph in (1, 4):
                    v = (mb + k) & 3
                    if ph == 1:
                        ops = [(A.at[n, :, v], B.at[n, pl.ds(mb * 4, 4)], dv(b, v, c), k == 0)]
                    else:
                        ops = [(B.at[n, pl.ds(v * 4, 4)], A.at[n, :, mb], dv(b, v, c), k == 0)]
                else:
                    v = (md + k) & 3
                    ops = []
                    for dc in range(2):
                        t = c ^ dc
                        here = k == 0 and dc == 0
                        if ph == 2:
                            ops.append(
                                (B.at[n, :, v * 2 + t], R.at[n, pl.ds((md * 2 + c) * 16, 16)], dv(d, v, t), here)
                            )
                        else:
                            ops.append(
                                (R.at[n, pl.ds((v * 2 + t) * 16, 16)], B.at[n, :, md * 2 + c], dv(d, v, t), here)
                            )
                for src, dst, dev, here in ops:
                    if here:
                        pltpu.make_async_copy(src, dst, lsem.at[ph, j, q]).start()
                    else:
                        remote(src, dst, ph, j, q, dev).start()

    def wait(ph, j):
        for q in range(3):
            if ph in (2, 3):
                far = R.at[0, pl.ds(0, 112)]
                near = R.at[0, pl.ds(0, 16)]
            else:
                far = R.at[0, pl.ds(0, 96)]
                near = R.at[0, pl.ds(0, 32)]
            pltpu.make_async_copy(far, far, rsem.at[ph, j, q]).wait()
            pltpu.make_async_copy(near, near, lsem.at[ph, j, q]).wait()
            pltpu.make_async_copy(far, far, ssem.at[ph, j, q]).wait()

    rows = lax.broadcasted_iota(jnp.int32, (256, 256), 0)
    cols = lax.broadcasted_iota(jnp.int32, (256, 256), 1)
    perm = jnp.where(cols == (rows & 15) * 16 + (rows >> 4), 1.0, 0.0).astype(BF)

    def experts(j):
        def unpack(i, carry):
            n = 3 * j + i // 8
            r0 = pl.multiple_of((i % 8) * 16, 16)
            x0 = pl.multiple_of(i * 16, 16)
            lo = R[n, pl.ds(r0, 16), :16, :].reshape(256, 128)
            hi = R[n, pl.ds(r0, 16), 16:, :].reshape(256, 128)
            out = jnp.dot(perm, jnp.concatenate([lo, hi], axis=1), preferred_element_type=F32).astype(BF)
            for u in range(16):
                X[pl.ds(x0, 16), u * 128 : (u + 1) * 128] = out[u * 16 : (u + 1) * 16, :128]
                X[pl.ds(x0, 16), 2048 + u * 128 : 2048 + (u + 1) * 128] = out[u * 16 : (u + 1) * 16, 128:]
            return carry

        lax.fori_loop(0, 24, unpack, 0)
        if j == 0:
            pltpu.make_async_copy(down_ref, D, dsem).wait()
        saved_copy(j).wait()

        def first(i, carry):
            at = pl.multiple_of(i * 256, 256)
            dg = lax.dot_general(
                X[...], D[pl.ds(at, 256), :], (((1,), (1,)), ((), ())), preferred_element_type=F32
            )
            gate = sv[:, :, pl.ds(at, 256)].reshape(384, 256).astype(F32)
            upper = sv[:, :, pl.ds(768 + at, 256)].reshape(384, 256).astype(F32)
            sigma = 1.0 / (1.0 + jnp.exp(-gate))
            ds = dg * sigma
            act[:, pl.ds(at, 256)] = (ds * upper * (1.0 + gate * (1.0 - sigma))).astype(BF)
            act[:, pl.ds(768 + at, 256)] = (ds * gate).astype(BF)
            return carry

        lax.fori_loop(0, 3, first, 0)
        if j < 2:
            saved_copy(j + 1).start()

        def second(i, carry):
            slot = i % 2
            gate_copy(i, slot).wait()
            at = pl.multiple_of(i * 512, 512)
            X[:, pl.ds(at, 512)] = lax.dot_general(
                act[...], G[slot], (((1,), (1,)), ((), ())), preferred_element_type=F32
            ).astype(BF)
            if j < 2:
                gate_copy((i + 2) % 8, slot).start()
            else:
                @pl.when(i < 6)
                def _():
                    gate_copy(i + 2, slot).start()
            return carry

        lax.fori_loop(0, 8, second, 0)

        def pack(i, carry):
            n = 3 * j + i // 8
            r0 = pl.multiple_of((i % 8) * 16, 16)
            x0 = pl.multiple_of(i * 16, 16)
            lo = jnp.concatenate([X[pl.ds(x0, 16), u * 128 : (u + 1) * 128] for u in range(16)], axis=0)
            hi = jnp.concatenate([X[pl.ds(x0, 16), 2048 + u * 128 : 2048 + (u + 1) * 128] for u in range(16)], axis=0)
            out = jnp.dot(perm, jnp.concatenate([lo, hi], axis=1), preferred_element_type=F32).astype(BF)
            R[n, pl.ds(r0, 16), :16, :] = out[:, :128].reshape(16, 16, 128)
            R[n, pl.ds(r0, 16), 16:, :] = out[:, 128:].reshape(16, 16, 128)
            return carry

        lax.fori_loop(0, 24, pack, 0)

    def kv_copies():
        for k in range(1, 8):
            to = (bme + k) & 7
            for src, dst, t in ((k_ref, kf_ref, 0), (v_ref, vf_ref, 1)):
                yield pltpu.make_async_remote_copy(
                    src, dst.at[bme], kvs.at[t], kvr.at[t], device_id=(to, eme), device_id_type=MESH
                )

    for step in range(9):
        active = [(ph, step - ph - (1 if ph >= 3 else 0)) for ph in range(6)]
        active = [(ph, j) for ph, j in active if 0 <= j < 3]
        for ph, j in active:
            phase(ph, j)
        if step == 0:
            kf_ref[bme] = k_ref[...]
            vf_ref[bme] = v_ref[...]
            for copy in kv_copies():
                copy.start()
            build(1)
            build(2)
        if 3 <= step < 6:
            experts(step - 3)
        for ph, j in active:
            wait(ph, j)

    for t, full in ((0, kf_ref), (1, vf_ref)):
        seven = full.at[pl.ds(0, 7)]
        pltpu.make_async_copy(seven, seven, kvr.at[t]).wait()
        pltpu.make_async_copy(seven, seven, kvs.at[t]).wait()

    def combine(t, carry):
        total = g_ref[t].astype(F32)
        for k in range(8):
            at = ret[t * 8 + k]
            total += wts[t * 8 + k] * S[at // 32, (at // 8) % 4, at % 8].astype(F32)
        res_ref[t] = total.astype(BF)
        return carry

    lax.fori_loop(0, 128, combine, 0)


def exchange(tok, ret, wts, g3, keys, values, saved, down, gate):
    smem = pl.BlockSpec(memory_space=pltpu.SMEM)
    vmem = pl.BlockSpec(memory_space=pltpu.VMEM)
    hbm = pl.BlockSpec(memory_space=pl.ANY)
    row = (32, 128)
    return pl.pallas_call(
        exchange_kernel,
        out_shape=(
            jax.ShapeDtypeStruct((128,) + row, BF),
            jax.ShapeDtypeStruct((8, 128, 256), BF),
            jax.ShapeDtypeStruct((8, 128, 256), BF),
        ),
        in_specs=[smem, smem, smem, vmem, vmem, vmem, hbm, hbm, hbm],
        out_specs=(vmem, vmem, vmem),
        scratch_shapes=[
            pltpu.VMEM((36, 4, 8) + row, BF),
            pltpu.VMEM((9, 4, 4, 8) + row, BF),
            pltpu.VMEM((9, 16, 8) + row, BF),
            pltpu.VMEM((9, 128) + row, BF),
            pltpu.VMEM((384, 4096), BF),
            pltpu.VMEM((384, 1536), BF),
            pltpu.VMEM((768, 4096), BF),
            pltpu.VMEM((2, 512, 1536), BF),
            pltpu.VMEM((3, 128, 1536), BF),
            pltpu.SemaphoreType.DMA((6, 3, 3)),
            pltpu.SemaphoreType.DMA((6, 3, 3)),
            pltpu.SemaphoreType.DMA((6, 3, 3)),
            pltpu.SemaphoreType.DMA((2,)),
            pltpu.SemaphoreType.DMA((2,)),
            pltpu.SemaphoreType.DMA,
            pltpu.SemaphoreType.DMA((2,)),
            pltpu.SemaphoreType.DMA,
        ],
        compiler_params=pltpu.CompilerParams(
            collective_id=0, has_side_effects=True, vmem_limit_bytes=63 << 20
        ),
    )(tok, ret, wts, g3, keys, values, saved, down, gate)


def attention_kernel(
    q_ref, res_ref, k_ref, v_ref, posq_ref, posk_ref,
    dq_ref, dk_out, dv_out,
    kt, vt, dk_acc, dv_acc, part, got, ssem, rsem,
):
    bme = lax.axis_index("blk")
    eme = lax.axis_index("expert")
    barrier = pltpu.get_barrier_semaphore()
    for k in range(1, 8):
        pl.semaphore_signal(barrier, inc=1, device_id=((bme + k) & 7, eme), device_id_type=MESH)
    scale = 1.0 / math.sqrt(HEAD)

    def copies(h):
        for k in range(1, 8):
            to = (bme + k) & 7
            yield pltpu.make_async_remote_copy(
                part.at[h, to], got.at[h, bme], ssem.at[h], rsem.at[h], device_id=(to, eme), device_id_type=MESH
            )

    for h in range(2):
        keys = k_ref[:, h * 128 : (h + 1) * 128]
        values = v_ref[:, h * 128 : (h + 1) * 128]
        kt[...] = keys.T
        vt[...] = values.T
        dk_acc[...] = jnp.zeros_like(dk_acc)
        dv_acc[...] = jnp.zeros_like(dv_acc)

        def tile(i, carry):
            t0 = pl.multiple_of(i * 16, 16)
            q = q_ref[pl.ds(t0, 16), h * 16 : (h + 1) * 16, :].reshape(256, 128)
            g = res_ref[pl.ds(t0, 16), h * 16 : (h + 1) * 16, :].reshape(256, 128)
            nt = (((1,), (1,)), ((), ()))
            scores = lax.dot_general(k_ref[:, h * 128 : (h + 1) * 128], q, nt, preferred_element_type=F32) * scale
            scores = jnp.where(posq_ref[pl.ds(i, 1), :] >= posk_ref[...], scores, -1e30)
            top = jnp.max(scores, axis=0, keepdims=True)
            weights = jnp.exp(scores - top)
            inverse = 1.0 / jnp.sum(weights, axis=0, keepdims=True)
            out = jnp.dot(vt[...], weights.astype(BF), preferred_element_type=F32) * inverse
            gt = g.astype(F32).T
            delta = jnp.sum(gt * out, axis=0, keepdims=True)
            probs = weights * inverse
            dv_acc[...] += jnp.dot(probs.astype(BF), g, preferred_element_type=F32)
            prob_grad = lax.dot_general(v_ref[:, h * 128 : (h + 1) * 128], g, nt, preferred_element_type=F32)
            score_grad = (probs * (prob_grad - delta)).astype(BF)
            dk_acc[...] += jnp.dot(score_grad, q, preferred_element_type=F32)
            dq = jnp.dot(kt[...], score_grad, preferred_element_type=F32) * scale
            dq_ref[pl.ds(t0, 16), h * 16 : (h + 1) * 16, :] = dq.T.astype(BF).reshape(16, 16, 128)
            return carry

        lax.fori_loop(0, 8, tile, 0)
        part[h, :, 0] = (dk_acc[...] * scale).astype(BF).reshape(8, 128, 128)
        part[h, :, 1] = dv_acc[...].astype(BF).reshape(8, 128, 128)
        got[h, bme] = part[h, bme]
        if h == 0:
            pl.semaphore_wait(barrier, 7)
        for copy in copies(h):
            copy.start()

    for h in range(2):
        seven = got.at[h, pl.ds(0, 7)]
        pltpu.make_async_copy(seven, seven, rsem.at[h]).wait()
        pltpu.make_async_copy(seven, seven, ssem.at[h]).wait()
        for t, out in ((0, dk_out), (1, dv_out)):
            total = got[h, 0, t].astype(F32)
            for s in range(1, 8):
                total += got[h, s, t].astype(F32)
            out[:, h * 128 : (h + 1) * 128] = total.astype(BF)


def attention(q3, res, keys, values, posq, posk):
    vmem = pl.BlockSpec(memory_space=pltpu.VMEM)
    return pl.pallas_call(
        attention_kernel,
        out_shape=(
            jax.ShapeDtypeStruct((128, 32, 128), BF),
            jax.ShapeDtypeStruct((128, 256), BF),
            jax.ShapeDtypeStruct((128, 256), BF),
        ),
        in_specs=[vmem] * 6,
        out_specs=(vmem,) * 3,
        scratch_shapes=[
            pltpu.VMEM((128, 1024), BF),
            pltpu.VMEM((128, 1024), BF),
            pltpu.VMEM((1024, 128), F32),
            pltpu.VMEM((1024, 128), F32),
            pltpu.VMEM((2, 8, 2, 128, 128), BF),
            pltpu.VMEM((2, 8, 2, 128, 128), BF),
            pltpu.SemaphoreType.DMA((2,)),
            pltpu.SemaphoreType.DMA((2,)),
        ],
        compiler_params=pltpu.CompilerParams(
            collective_id=1, has_side_effects=True, vmem_limit_bytes=40 << 20
        ),
    )(q3, res, keys, values, posq, posk)


def tables(ids):
    experts = jnp.arange(128, dtype=jnp.int32)
    match = ids[:, :, None] == experts
    named = jnp.any(match, axis=1)
    lower = (experts[:, None] > experts[None, :]).astype(BF)
    rank = jnp.dot(lower, named.astype(BF), preferred_element_type=F32).astype(jnp.int32)
    slots = jnp.arange(9, dtype=jnp.int32)
    hit = named[None] & (rank[None] == slots[:, None, None])
    tok = 128 + jnp.sum(jnp.where(hit, experts[None, :, None] - 128, 0), axis=1)
    tok = tok.reshape(3, 3, 4, 4, 4, 2)
    tok = jnp.stack(
        [
            tok[:, 0].transpose(0, 3, 1, 2, 4),
            tok[:, 1],
            tok[:, 2].transpose(0, 2, 3, 1, 4),
        ],
        axis=1,
    ).reshape(-1)
    slot = jnp.sum(jnp.where(match, rank[:, None, :], 0), axis=-1)
    y, z, x, c = ids // 32, (ids // 8) % 4, (ids // 2) % 4, ids % 2
    q = slot % 3
    place = jnp.where(
        q == 0,
        x * 32 + y * 8 + z * 2,
        jnp.where(q == 1, y * 32 + z * 8 + x * 2, z * 32 + x * 8 + y * 2),
    )
    ret = slot * 128 + place + c
    return tok, ret.reshape(-1)


def local(query, keys, values, grad_output, expert_ids, gate_weights, gate_up, down_weight, saved_preact, block_order):
    tok, ret = tables(expert_ids[0])
    g3 = jnp.pad(grad_output[0].reshape(128, 32, 128), ((0, 1), (0, 0), (0, 0)))
    s = saved_preact[0].reshape(4, 4, 4, 2, 3, 3, 1536)
    saved = jnp.stack(
        [
            s[..., 0, :].transpose(4, 1, 3, 0, 2, 5),
            s[..., 1, :].transpose(4, 2, 3, 1, 0, 5),
            s[..., 2, :].transpose(4, 0, 3, 2, 1, 5),
        ],
        axis=1,
    ).reshape(9, 128, 1536)
    res, kf, vf = exchange(
        tok, ret, gate_weights[0].reshape(-1), g3, keys[0], values[0], saved, down_weight[0], gate_up[0]
    )
    all_rows = jnp.arange(1024, dtype=jnp.int32)
    position = block_order[all_rows // 64] * 64 + all_rows % 64
    own = lax.dynamic_slice(position, (lax.axis_index("blk") * 128,), (128,))
    posq = jnp.repeat(own, 16).reshape(8, 256)
    dq, dk, dv = attention(
        query[0].reshape(128, 32, 128), res, kf.reshape(1024, 256), vf.reshape(1024, 256), posq, position[:, None]
    )
    return dq.reshape(1, 128, 4096), dk[None], dv[None]


def solution(mesh):
    token = P("expert", "blk", None)
    owner = P(("blk", "expert"), None, None)
    in_specs = (token,) * 6 + (owner, owner, P(("blk", "expert"), None, None, None), P())
    return jax.shard_map(local, mesh=mesh, in_specs=in_specs, out_specs=(token,) * 3, check_vma=False)
```

time: 955 us -> 346 us (0.36)
  Pallas kernels: 0 us -> 290 us
  blocking collectives: 279 us -> 0 us
  waiting for transfers between devices: 217 us -> 0 us
  local copies, waits for them, and re-layouts: 161 us -> 32.2 us
  other arithmetic: 131 us -> 19.5 us
  matrix products: 95.7 us -> 0.15 us
  starting transfers between devices: 57.2 us -> 0 us
    pallas_call x0 -> x2, Pallas kernels: none -> 290 us  [the longest x1 257 us: exchange(): pl.pallas_call(exchange_kernel, out_shape=(jax.ShapeDtypeStruct((128,) +...]
    all_gather x2 -> x0, blocking collectives: 279 us -> none  [the longest x1 248 us: local(): value_piece = lax.all_gather(values[0], 'blk', axis=0, tiled=True)]
    all_to_all x2 -> x0, waiting for transfers between devices: 192 us -> none  [the longest x1 192 us: local(): lax.all_to_all(outgoing, ('blk', 'expert'), split_axis=0, concat_axis=0,...]
    dot_general x44 -> x1, matrix products: 95.7 us -> 0.15 us  [tables(): jnp.dot(lower, named.astype(BF), preferred_element_type=F32)]
    add x11 -> x4, other arithmetic: 97.2 us -> 6.38 us  [the longest x2 5.75 us: local(): position = block_order[all_rows // 64] * 64 + all_rows % 64]
    reshape x4 -> x3, local copies, waits for them, and re-layouts: 61.9 us -> 8.94 us  [the longest x1 6.8 us: local(): saved = jnp.stack([s[..., 0, :].transpose(4, 1, 3, 0, 2, 5), s[..., 1, :]...]
    all_to_all x2 -> x0, starting transfers between devices: 33.5 us -> none  [the longest x1 22.9 us: local(): lax.all_to_all(expert_back, ('blk', 'expert'), split_axis=0, concat_axis=...]
    gather x11 -> x1, local copies, waits for them, and re-layouts: 34.4 us -> 1.96 us  [local(): position = block_order[all_rows // 64] * 64 + all_rows % 64]
  transfers between devices with their start and end apart: 18 -> 0, of which waited for: 9 -> 0; matrix products, arithmetic and copies ran while one was open for 22% -> 0% of each run, Pallas kernels for 0% -> 0%
where the time goes in v1:
time: 346 us; the launch traced here: 343 us
  Pallas kernels  290 us (84%)
  local copies, waits for them, and re-layouts  32.2 us (9%)
  other arithmetic  19.5 us (6%)
    pallas_call x1, Pallas kernels, exchange(): pl.pallas_call(exchange_kernel, out_shape=(jax.ShapeDtypeStruct((128,) +...  257 us
    pallas_call x1, Pallas kernels, attention(): pl.pallas_call(attention_kernel, out_shape=(jax.ShapeDtypeStruct((128, 32...  33.2 us
    another operation x1, local copies, waits for them, and re-layouts, local(): s = saved_preact[0].reshape(4, 4, 4, 2, 3, 3, 1536)  8.09 us

profile of v1, /device:TPU:36, one launch (start us, length us, event | category | flops | bytes accessed | tf_op | source)
XLA Modules:
  0.0 342.7 jit_solution(14301201070460019749)
XLA Ops:
  0.6 2.0 fusion.50
  2.6 4.6 %select_reduce_fusion.1 = s32[1024]{0:T(1024)S(1)} fusion(s32[]{:T(128)} %bitcast.31, s32[]{:T(128)} %bitcast.32, s32[]{:T(128)} %bitcast.33, s32[]{:T(128)} %bitcast.34, s32[]{:T(128)} %bitcast.35, s32[]{:T(128)} %bitcast.37, s32[]{:T(128)} %bitcast.36), kind=kLoop, calls=%fused_computation.36 | loop fusion | flops 23552 | bytes 4124 | tf_op jit(solution)/shard_map/gather | solution.py:420
  7.2 0.2 fusion.25
  7.3 0.2 fusion.26
  7.5 0.2 fusion.27
  7.7 0.2 fusion.28
  7.9 0.2 fusion.29
  8.1 0.2 fusion.30
  8.3 0.2 fusion.31
  8.4 0.2 fusion.32
  8.6 0.2 fusion.33
  8.8 5.7 %fusion.39 = (s32[1024]{0:T(1024)S(1)}, s32[1024]{0:T(1024)S(1)}) fusion(pred[1024]{0:T(1024)(128)(4,1)S(1)} %fusion.25, pred[1024]{0:T(1024)(128)(4,1)S(1)} %fusion.26, pred[1024]{0:T(1024)(128)(4,1)S(1)} %fusion.33, pred[1024]{0:T(1024)(128)(4,1)S(1)} %fusion.32, pred[1024]{0:T(1024)(128)(4,1)S(1)} %fusion.31, pred[1024]{0:T(1024)(128)(4,1)S(1)} %fusion.30, ...), kind=kLoop, calls=%fused_computation.79 | loop fusion | flops 17408 | bytes 21540 | tf_op jit(solution)/shard_map/add | solution.py:420
  14.5 0.2 copy.38
  14.8 0.1 dynamic_slice.3
  14.9 0.1 broadcast_in_dim.51
  14.9 0.1 broadcast_in_dim.52
  15.0 0.1 broadcast_in_dim.53.posq_ref
  15.1 0.1 copy.29
  15.2 0.3 fusion.24
  15.5 0.1 convolution_convert_fusion
  15.7 0.2 select_reduce_fusion
  15.8 0.4 add.131
  16.4 0.1 copy.32
  16.5 0.9 reshape.114.tok
  17.4 2.4 select_reduce_fusion.2
  19.8 0.1 mul.65
  19.9 0.1 rem.112
  20.0 0.1 copy.33
  20.1 0.1 squeeze.32
  20.2 0.6 fusion.38.ret
  20.8 8.1 %reshape_squeeze.15 = bf16[4,4,4,2,3,3,1536]{6,3,2,1,0,5,4:T(2,128)(2,1)} reshape(bf16[1,128,9,1536]{3,1,2,0:T(8,128)(2,1)} %param.18) | data formatting | bytes 7077888 | tf_op jit(solution)/shard_map/reshape;squeeze | solution.py:407
  28.9 4.3 %fusion.48 = (bf16[4,4,4,2,3,1,1536]{6,3,2,1,0,5,4:T(2,128)(2,1)S(1)}, bf16[4,4,4,2,3,1,1536]{6,3,2,1,0,5,4:T(2,128)(2,1)S(1)}, bf16[4,4,4,2,3,1,1536]{6,3,2,1,0,5,4:T(2,128)(2,1)S(1)}) fusion(bf16[4,4,4,2,3,3,1536]{6,3,2,1,0,5,4:T(2,128)(2,1)} %reshape_squeeze.15), kind=kLoop, calls=%fused_computation.93 | loop fusion | bytes 7077888 | tf_op jit(solution)/shard_map/slice | solution.py:410
  33.2 0.6 copy.50
  33.8 0.9 copy.51
  34.7 0.6 copy.52
  35.3 4.0 %pad_maximum_fusion = bf16[3,3,4,2,4,4,1536]{6,5,4,3,2,1,0:T(4,128)(2,1)} fusion(bf16[3,1,4,2,4,4,1536]{6,5,4,3,2,1,0:T(4,128)(2,1)S(1)} %bitcast.78, bf16[3,1,4,2,4,4,1536]{6,5,4,3,2,1,0:T(4,128)(2,1)S(1)} %bitcast.79, bf16[3,1,4,2,4,4,1536]{6,5,4,3,2,1,0:T(4,128)(2,1)S(1)} %bitcast.80), kind=kLoop, calls=%fused_computation | loop fusion | flops 3538944 | bytes 7077888 | tf_op jit(solution)/shard_map/stack | solution.py:408
  39.3 6.8 %reshape.115.saved_ref = bf16[9,128,1536]{2,1,0:T(8,128)(2,1)} reshape(bf16[3,3,4,2,4,4,1536]{6,5,4,3,2,1,0:T(4,128)(2,1)} %pad_maximum_fusion) | data formatting | bytes 7077888 | tf_op jit(solution)/shard_map/reshape | solution.py:415
  46.1 0.2 copy.45
  46.4 1.2 pad.4.g_ref
  47.6 0.1 copy.34
  47.7 0.7 reshape_squeeze.13.wts
  48.4 256.8 %shard_map.121 = (bf16[128,32,128]{2,1,0:T(8,128)(2,1)}, bf16[8,128,256]{2,1,0:T(8,128)(2,1)}, bf16[8,128,256]{2,1,0:T(8,128)(2,1)}) custom-call(s32[1152]{0:T(1024)} %reshape.114.tok, s32[1024]{0:T(1024)} %fusion.38.ret, f32[1024]{0:T(1024)} %reshape_squeeze.13.wts, bf16[129,32,128]{2,1,0:T(8,128)(2,1)} %pad.4.g_ref, bf16[128,256]{1,0:T(8,128)(2,1)} %bitcast.85, ...), custom_call_target="tpu_custom_call" | custom-call | tf_op jit(solution)/shard_map/pallas_call | solution.py:244
  305.2 1.6 copy.44
  306.8 0.2 copy-done.2
  307.0 33.2 %shard_map.122 = (bf16[128,32,128]{2,1,0:T(8,128)(2,1)S(1)}, bf16[128,256]{1,0:T(8,128)(2,1)S(1)}, bf16[128,256]{1,0:T(8,128)(2,1)S(1)}) custom-call(bf16[128,32,128]{2,1,0:T(8,128)(2,1)S(1)} %bitcast.71, bf16[128,32,128]{2,1,0:T(8,128)(2,1)S(1)} %copy-done, bf16[1024,256]{1,0:T(8,128)(2,1)S(1)} %bitcast.72, bf16[1024,256]{1,0:T(8,128)(2,1)S(1)} %bitcast.73, ...), custom_call_target="tpu_custom_call" | custom-call | tf_op jit(solution)/shard_map/pallas_call | solution.py:349
  340.2 1.3 reshape.118
  341.5 0.6 copy.56
  342.1 0.6 copy.57
  (19 shorter events, 0.3 us)
Async XLA Ops:
  0.6 14.5 %copy-start.4 = (s32[1,128,8]{1,2,0:T(8,128)S(1)}, s32[1,128,8]{1,2,0:T(8,128)}, u32[]{:S(2)}) copy-start(s32[1,128,8]{1,2,0:T(8,128)} %param.14) | copy-start | bytes 12292
  39.3 6.8 %copy-start.3 = (bf16[1,128,4096]{2,1,0:T(8,128)(2,1)S(1)}, bf16[1,128,4096]{2,1,0:T(8,128)(2,1)}, u32[]{:S(2)}) copy-start(bf16[1,128,4096]{2,1,0:T(8,128)(2,1)} %param.13) | copy-start | bytes 3145732
  46.4 1.2 copy-start.5
  305.2 1.6 copy-start
  305.2 1.7 copy-start.1
  305.2 1.8 copy-start.2

commit v2 on v1

v2 whole, which is shorter than its diff:
```python
import math

import jax
import jax.numpy as jnp
from jax import lax
from jax.experimental import pallas as pl
from jax.experimental.pallas import tpu as pltpu
from jax.sharding import PartitionSpec as P

MESH = pl.DeviceIdType.MESH
HEAD = 128
ORDERS = ((0, 1, 2), (1, 2, 0), (2, 0, 1))
BF = jnp.bfloat16
F32 = jnp.float32
GB = 256


def coords():
    b = lax.axis_index("blk")
    e = lax.axis_index("expert")
    return (e // 2) % 4, b // 2, (b % 2) * 2 + e // 8, e % 2


def device_of(x, y, z, c):
    return (y * 2 + z // 2, ((z % 2) * 4 + x) * 2 + c)


def place_expert(q, lane):
    a, b, d = ORDERS[q]
    t = [None] * 3
    t[a], t[b], t[d] = lane >> 5, (lane >> 3) & 3, (lane >> 1) & 3
    return t[1] * 32 + t[2] * 8 + t[0] * 2 + (lane & 1)


def exchange_kernel(
    ids_ref, wts_ref, g_ref, k_ref, v_ref, saved_ref, down_ref, gate_ref,
    res_ref, kf_ref, vf_ref,
    S, A, B, R, X, act, D, G, sv, acc, rank_ref, mix_ref, order_ref,
    ssem, rsem, lsem, kvs, kvr, dsem, gsem, svsem,
):
    x, y, z, c = coords()
    cc = (x, y, z)
    bme = lax.axis_index("blk")
    eme = lax.axis_index("expert")

    def dv(dim, v, core):
        t = [x, y, z]
        t[dim] = v
        return device_of(t[0], t[1], t[2], core)

    barrier = pltpu.get_barrier_semaphore()
    peers = [dv(dim, (cc[dim] + k) & 3, c ^ dc) for dim in range(3) for k in range(1, 4) for dc in range(2)]
    peers.append(dv(0, x, c ^ 1))
    peers += [device_of(x, (y + k) & 3, z ^ 2, c) for k in range(1, 4)]
    for p in peers:
        pl.semaphore_signal(barrier, inc=1, device_id=p, device_id_type=MESH)

    pltpu.make_async_copy(down_ref, D, dsem).start()

    def gate_copy(block, slot):
        return pltpu.make_async_copy(gate_ref.at[pl.ds(block * GB, GB)], G.at[slot], gsem.at[slot])

    gate_copy(0, 0).start()
    gate_copy(1, 1).start()

    sub = lax.broadcasted_iota(jnp.int32, (128, 128), 0)
    lane = lax.broadcasted_iota(jnp.int32, (128, 128), 1)
    upper_half = jnp.where(sub < lane, 1.0, 0.0).astype(BF)
    for q in range(3):
        expert = place_expert(q, sub)
        named = jnp.zeros((128, 128), F32)
        mix = jnp.zeros((128, 128), F32)
        for k in range(8):
            match = ids_ref[k : k + 1, :] == expert
            named += jnp.where(match, 1.0, 0.0)
            mix += jnp.where(match, wts_ref[k : k + 1, :], 0.0)
        rank = jnp.dot(named.astype(BF), upper_half, preferred_element_type=F32)
        rank_ref[q] = jnp.where(named > 0.5, rank, -1.0)
        mix_ref[q] = mix

    rows = lax.broadcasted_iota(jnp.int32, (256, 256), 0)
    cols = lax.broadcasted_iota(jnp.int32, (256, 256), 1)
    perm = jnp.where(cols == (rows & 15) * 16 + (rows >> 4), 1.0, 0.0).astype(BF)

    def unpacked(lo, hi, x0):
        out = jnp.dot(perm, jnp.concatenate([lo, hi], axis=1), preferred_element_type=F32).astype(BF)
        for u in range(16):
            X[pl.ds(x0, 16), u * 128 : (u + 1) * 128] = out[u * 16 : (u + 1) * 16, :128]
            X[pl.ds(x0, 16), 2048 + u * 128 : 2048 + (u + 1) * 128] = out[u * 16 : (u + 1) * 16, 128:]

    def packed(x0):
        lo = jnp.concatenate([X[pl.ds(x0, 16), u * 128 : (u + 1) * 128] for u in range(16)], axis=0)
        hi = jnp.concatenate([X[pl.ds(x0, 16), 2048 + u * 128 : 2048 + (u + 1) * 128] for u in range(16)], axis=0)
        return jnp.dot(perm, jnp.concatenate([lo, hi], axis=1), preferred_element_type=F32).astype(BF)

    def build(j):
        for q in range(3):
            pick = jnp.where(rank_ref[q] == float(3 * j + q), 1.0, 0.0).astype(BF)
            for h in range(4):
                X[q * 128 : (q + 1) * 128, h * 1024 : (h + 1) * 1024] = jnp.dot(
                    pick, g_ref[:, h * 1024 : (h + 1) * 1024], preferred_element_type=F32
                ).astype(BF)

        def body(i, carry):
            out = packed(pl.multiple_of(i * 16, 16))
            at = j * 12 + i // 2
            S[at, pl.ds(i % 2 * 2, 2), :, :16, :] = out[:, :128].reshape(2, 8, 16, 128)
            S[at, pl.ds(i % 2 * 2, 2), :, 16:, :] = out[:, 128:].reshape(2, 8, 16, 128)
            return carry

        lax.fori_loop(0, 24, body, 0)

    def combine(j):
        def body(i, carry):
            at = j * 12 + i // 2
            lo = S[at, pl.ds(i % 2 * 2, 2), :, :16, :].reshape(256, 128)
            hi = S[at, pl.ds(i % 2 * 2, 2), :, 16:, :].reshape(256, 128)
            unpacked(lo, hi, pl.multiple_of(i * 16, 16))
            return carry

        lax.fori_loop(0, 24, body, 0)
        mix = jnp.concatenate(
            [jnp.where(rank_ref[q] == float(3 * j + q), mix_ref[q], 0.0) for q in range(3)], axis=0
        ).T.astype(BF)
        for h in range(4):
            cut = slice(h * 1024, (h + 1) * 1024)
            before = g_ref[:, cut].astype(F32) if j == 0 else acc[:, cut]
            total = before + jnp.dot(mix, X[:, cut], preferred_element_type=F32)
            if j < 2:
                acc[:, cut] = total
            else:
                res_ref[:, cut] = total.astype(BF)

    def saved_copy(j):
        return pltpu.make_async_copy(saved_ref.at[pl.ds(3 * j, 3)], sv, svsem)

    saved_copy(0).start()

    for q in range(3):
        a, b, d = ORDERS[q]
        t = [None] * 3
        t[a], t[b], t[d] = sub & 3, (sub >> 2) & 3, sub >> 5
        source = t[1] * 32 + t[2] * 8 + t[0] * 2 + ((sub >> 4) & 1)
        order_ref[q] = jnp.where(lane == source, 1.0, 0.0).astype(BF)

    build(0)
    pl.semaphore_wait(barrier, len(peers))

    def remote(src, dst, ph, j, q, dev):
        return pltpu.make_async_remote_copy(
            src, dst, ssem.at[ph, j, q], rsem.at[ph, j, q], device_id=dev, device_id_type=MESH
        )

    def phase(ph, j, q):
        a, b, d = ORDERS[q]
        ma, mb, md = cc[a], cc[b], cc[d]
        n = 3 * j + q
        for k in (2, 1, 3, 0):
            if ph in (0, 5):
                v = (ma + k) & 3
                if ph == 0:
                    ops = [(S.at[n * 4 + v], A.at[n, ma], dv(a, v, c), k == 0)]
                else:
                    ops = [(A.at[n, v], S.at[n * 4 + ma], dv(a, v, c), k == 0)]
            elif ph in (1, 4):
                v = (mb + k) & 3
                if ph == 1:
                    ops = [(A.at[n, :, v], B.at[n, pl.ds(mb * 4, 4)], dv(b, v, c), k == 0)]
                else:
                    ops = [(B.at[n, pl.ds(v * 4, 4)], A.at[n, :, mb], dv(b, v, c), k == 0)]
            else:
                v = (md + k) & 3
                ops = []
                for dc in range(2):
                    t = c ^ dc
                    here = k == 0 and dc == 0
                    if ph == 2:
                        ops.append((B.at[n, :, v * 2 + t], R.at[n, pl.ds((md * 2 + c) * 16, 16)], dv(d, v, t), here))
                    else:
                        ops.append((R.at[n, pl.ds((v * 2 + t) * 16, 16)], B.at[n, :, md * 2 + c], dv(d, v, t), here))
            for src, dst, dev, here in ops:
                if here:
                    pltpu.make_async_copy(src, dst, lsem.at[ph, j, q]).start()
                else:
                    remote(src, dst, ph, j, q, dev).start()

    def wait(ph, j, q):
        mine = 16 if ph in (2, 3) else 32
        far = R.at[0, pl.ds(0, 128 - mine)]
        near = R.at[0, pl.ds(0, mine)]
        pltpu.make_async_copy(far, far, rsem.at[ph, j, q]).wait()
        pltpu.make_async_copy(near, near, lsem.at[ph, j, q]).wait()
        pltpu.make_async_copy(far, far, ssem.at[ph, j, q]).wait()

    def experts(j):
        def unpack(i, carry):
            n = 3 * j + i // 8
            r0 = pl.multiple_of((i % 8) * 16, 16)
            lo = R[n, pl.ds(r0, 16), :16, :].reshape(256, 128)
            hi = R[n, pl.ds(r0, 16), 16:, :].reshape(256, 128)
            unpacked(lo, hi, pl.multiple_of(i * 16, 16))
            return carry

        lax.fori_loop(0, 24, unpack, 0)
        if j == 0:
            pltpu.make_async_copy(down_ref, D, dsem).wait()

        def first(i, carry):
            at = pl.multiple_of(i * 256, 256)
            dg = lax.dot_general(
                X[...], D[pl.ds(at, 256), :], (((1,), (1,)), ((), ())), preferred_element_type=F32
            )
            for q in range(3):
                cut = slice(q * 128, (q + 1) * 128)
                gate = jnp.dot(order_ref[q], sv[q, :, pl.ds(at, 256)], preferred_element_type=F32)
                upper = jnp.dot(order_ref[q], sv[q, :, pl.ds(768 + at, 256)], preferred_element_type=F32)
                sigma = 1.0 / (1.0 + jnp.exp(-gate))
                ds = dg[cut] * sigma
                act[cut, pl.ds(at, 256)] = (ds * upper * (1.0 + gate * (1.0 - sigma))).astype(BF)
                act[cut, pl.ds(768 + at, 256)] = (ds * gate).astype(BF)
            return carry

        saved_copy(j).wait()
        lax.fori_loop(0, 3, first, 0)
        if j < 2:
            saved_copy(j + 1).start()
        blocks = 4096 // GB

        def second(i, carry):
            slot = i % 2
            gate_copy(i, slot).wait()
            at = pl.multiple_of(i * GB, GB)
            X[:, pl.ds(at, GB)] = lax.dot_general(
                act[...], G[slot], (((1,), (1,)), ((), ())), preferred_element_type=F32
            ).astype(BF)
            if j < 2:
                gate_copy((i + 2) % blocks, slot).start()
            else:
                @pl.when(i < blocks - 2)
                def _():
                    gate_copy(i + 2, slot).start()
            return carry

        lax.fori_loop(0, blocks, second, 0)

        def pack(i, carry):
            n = 3 * j + i // 8
            r0 = pl.multiple_of((i % 8) * 16, 16)
            out = packed(pl.multiple_of(i * 16, 16))
            R[n, pl.ds(r0, 16), :16, :] = out[:, :128].reshape(16, 16, 128)
            R[n, pl.ds(r0, 16), 16:, :] = out[:, 128:].reshape(16, 16, 128)
            return carry

        lax.fori_loop(0, 24, pack, 0)

    def each(ph, j):
        for q in range(3):
            phase(ph, j, q)

    def onward(ph, j):
        for q in range(3):
            wait(ph, j, q)
            if ph not in (2, 5):
                phase(ph + 1, j, q)

    each(0, 0)
    kf_ref[bme] = k_ref[...]
    vf_ref[bme] = v_ref[...]
    for k in range(1, 8):
        to = (bme + k) & 7
        for src, dst, t in ((k_ref, kf_ref, 0), (v_ref, vf_ref, 1)):
            pltpu.make_async_remote_copy(
                src, dst.at[bme], kvs.at[t], kvr.at[t], device_id=(to, eme), device_id_type=MESH
            ).start()
    build(1)
    onward(0, 0)
    each(0, 1)
    build(2)
    onward(1, 0)
    onward(0, 1)
    each(0, 2)
    onward(2, 0)
    onward(1, 1)
    onward(0, 2)
    experts(0)
    onward(2, 1)
    onward(1, 2)
    each(3, 0)
    experts(1)
    onward(3, 0)
    onward(2, 2)
    each(3, 1)
    experts(2)
    onward(4, 0)
    onward(3, 1)
    each(3, 2)
    onward(5, 0)
    combine(0)
    onward(4, 1)
    onward(3, 2)
    onward(4, 2)
    onward(5, 1)
    combine(1)
    onward(5, 2)
    combine(2)

    for t, full in ((0, kf_ref), (1, vf_ref)):
        seven = full.at[pl.ds(0, 7)]
        pltpu.make_async_copy(seven, seven, kvr.at[t]).wait()
        pltpu.make_async_copy(seven, seven, kvs.at[t]).wait()


def exchange(ids, wts, g, keys, values, saved, down, gate):
    vmem = pl.BlockSpec(memory_space=pltpu.VMEM)
    hbm = pl.BlockSpec(memory_space=pl.ANY)
    row = (32, 128)
    return pl.pallas_call(
        exchange_kernel,
        out_shape=(
            jax.ShapeDtypeStruct((128, 4096), BF),
            jax.ShapeDtypeStruct((8, 128, 256), BF),
            jax.ShapeDtypeStruct((8, 128, 256), BF),
        ),
        in_specs=[vmem] * 5 + [hbm] * 3,
        out_specs=(vmem, vmem, vmem),
        scratch_shapes=[
            pltpu.VMEM((36, 4, 8) + row, BF),
            pltpu.VMEM((9, 4, 4, 8) + row, BF),
            pltpu.VMEM((9, 16, 8) + row, BF),
            pltpu.VMEM((9, 128) + row, BF),
            pltpu.VMEM((384, 4096), BF),
            pltpu.VMEM((384, 1536), BF),
            pltpu.VMEM((768, 4096), BF),
            pltpu.VMEM((2, GB, 1536), BF),
            pltpu.VMEM((3, 128, 1536), BF),
            pltpu.VMEM((128, 4096), F32),
            pltpu.VMEM((3, 128, 128), F32),
            pltpu.VMEM((3, 128, 128), F32),
            pltpu.VMEM((3, 128, 128), BF),
            pltpu.SemaphoreType.DMA((6, 3, 3)),
            pltpu.SemaphoreType.DMA((6, 3, 3)),
            pltpu.SemaphoreType.DMA((6, 3, 3)),
            pltpu.SemaphoreType.DMA((2,)),
            pltpu.SemaphoreType.DMA((2,)),
            pltpu.SemaphoreType.DMA,
            pltpu.SemaphoreType.DMA((2,)),
            pltpu.SemaphoreType.DMA,
        ],
        compiler_params=pltpu.CompilerParams(
            collective_id=0, has_side_effects=True, vmem_limit_bytes=63 << 20
        ),
    )(ids, wts, g, keys, values, saved, down, gate)


def attention_kernel(
    order_ref, q_ref, res_ref, k_ref, v_ref,
    dq_ref, dk_out, dv_out,
    posk_ref, kt, vt, dk_acc, dv_acc, part, got, ssem, rsem,
):
    bme = lax.axis_index("blk")
    eme = lax.axis_index("expert")
    barrier = pltpu.get_barrier_semaphore()
    for k in range(1, 8):
        pl.semaphore_signal(barrier, inc=1, device_id=((bme + k) & 7, eme), device_id_type=MESH)
    scale = 1.0 / math.sqrt(HEAD)
    within = lax.broadcasted_iota(jnp.int32, (64, 1), 0)
    for i in range(16):
        posk_ref[i * 64 : (i + 1) * 64, :] = order_ref[i] * 64 + within
    lanes = lax.broadcasted_iota(jnp.int32, (1, 256), 1) & 127
    posq = jnp.where(lanes < 64, order_ref[2 * bme] * 64, order_ref[2 * bme + 1] * 64) + (lanes & 63)

    def copies(h):
        for k in range(1, 8):
            to = (bme + k) & 7
            yield pltpu.make_async_remote_copy(
                part.at[h, to], got.at[h, bme], ssem.at[h], rsem.at[h], device_id=(to, eme), device_id_type=MESH
            )

    for h in range(2):
        keys = k_ref[:, h * 128 : (h + 1) * 128]
        values = v_ref[:, h * 128 : (h + 1) * 128]
        kt[...] = keys.T
        vt[...] = values.T
        dk_acc[...] = jnp.zeros_like(dk_acc)
        dv_acc[...] = jnp.zeros_like(dv_acc)

        def tile(i, carry):
            one = pl.ds(pl.multiple_of((h * 16 + 2 * i) * 128, 128), 128)
            two = pl.ds(pl.multiple_of((h * 16 + 2 * i + 1) * 128, 128), 128)
            q = jnp.concatenate([q_ref[:, one], q_ref[:, two]], axis=0)
            g = jnp.concatenate([res_ref[:, one], res_ref[:, two]], axis=0)
            nt = (((1,), (1,)), ((), ()))
            scores = lax.dot_general(k_ref[:, h * 128 : (h + 1) * 128], q, nt, preferred_element_type=F32) * scale
            scores = jnp.where(posq >= posk_ref[...], scores, -1e30)
            top = jnp.max(scores, axis=0, keepdims=True)
            weights = jnp.exp(scores - top)
            inverse = 1.0 / jnp.sum(weights, axis=0, keepdims=True)
            out = jnp.dot(vt[...], weights.astype(BF), preferred_element_type=F32) * inverse
            delta = jnp.sum(g.astype(F32).T * out, axis=0, keepdims=True)
            probs = weights * inverse
            dv_acc[...] += jnp.dot(probs.astype(BF), g, preferred_element_type=F32)
            prob_grad = lax.dot_general(v_ref[:, h * 128 : (h + 1) * 128], g, nt, preferred_element_type=F32)
            score_grad = (probs * (prob_grad - delta)).astype(BF)
            dk_acc[...] += jnp.dot(score_grad, q, preferred_element_type=F32)
            dq = (jnp.dot(kt[...], score_grad, preferred_element_type=F32) * scale).T.astype(BF)
            dq_ref[:, one] = dq[:128]
            dq_ref[:, two] = dq[128:]
            return carry

        lax.fori_loop(0, 8, tile, 0)
        part[h, :, 0] = (dk_acc[...] * scale).astype(BF).reshape(8, 128, 128)
        part[h, :, 1] = dv_acc[...].astype(BF).reshape(8, 128, 128)
        got[h, bme] = part[h, bme]
        if h == 0:
            pl.semaphore_wait(barrier, 7)
        for copy in copies(h):
            copy.start()

    for h in range(2):
        seven = got.at[h, pl.ds(0, 7)]
        pltpu.make_async_copy(seven, seven, rsem.at[h]).wait()
        pltpu.make_async_copy(seven, seven, ssem.at[h]).wait()
        for t, out in ((0, dk_out), (1, dv_out)):
            total = got[h, 0, t].astype(F32)
            for s in range(1, 8):
                total += got[h, s, t].astype(F32)
            out[:, h * 128 : (h + 1) * 128] = total.astype(BF)


def attention(order, query, res, keys, values):
    vmem = pl.BlockSpec(memory_space=pltpu.VMEM)
    return pl.pallas_call(
        attention_kernel,
        out_shape=(
            jax.ShapeDtypeStruct((128, 4096), BF),
            jax.ShapeDtypeStruct((128, 256), BF),
            jax.ShapeDtypeStruct((128, 256), BF),
        ),
        in_specs=[pl.BlockSpec(memory_space=pltpu.SMEM)] + [vmem] * 4,
        out_specs=(vmem,) * 3,
        scratch_shapes=[
            pltpu.VMEM((1024, 1), jnp.int32),
            pltpu.VMEM((128, 1024), BF),
            pltpu.VMEM((128, 1024), BF),
            pltpu.VMEM((1024, 128), F32),
            pltpu.VMEM((1024, 128), F32),
            pltpu.VMEM((2, 8, 2, 128, 128), BF),
            pltpu.VMEM((2, 8, 2, 128, 128), BF),
            pltpu.SemaphoreType.DMA((2,)),
            pltpu.SemaphoreType.DMA((2,)),
        ],
        compiler_params=pltpu.CompilerParams(
            collective_id=1, has_side_effects=True, vmem_limit_bytes=40 << 20
        ),
    )(order, query, res, keys, values)


def local(query, keys, values, grad_output, expert_ids, gate_weights, gate_up, down_weight, saved_preact, block_order):
    res, kf, vf = exchange(
        expert_ids[0].T,
        gate_weights[0].T,
        grad_output[0],
        keys[0],
        values[0],
        saved_preact[0].transpose(1, 0, 2),
        down_weight[0],
        gate_up[0],
    )
    dq, dk, dv = attention(block_order, query[0], res, kf.reshape(1024, 256), vf.reshape(1024, 256))
    return dq[None], dk[None], dv[None]


def solution(mesh):
    token = P("expert", "blk", None)
    owner = P(("blk", "expert"), None, None)
    in_specs = (token,) * 6 + (owner, owner, P(("blk", "expert"), None, None, None), P())
    return jax.shard_map(local, mesh=mesh, in_specs=in_specs, out_specs=(token,) * 3, check_vma=False)
```

time: 346 us -> 288 us (0.83)
  local copies, waits for them, and re-layouts: 32.2 us -> 6.76 us
  other arithmetic: 19.5 us -> 0 us
  Pallas kernels: 290 us -> 278 us
    pallas_call x2, Pallas kernels: 290 us -> 278 us  [the longest x1 244 us: exchange(): pl.pallas_call(exchange_kernel, out_shape=(jax.ShapeDtypeStruct((128, 409...]
    reshape x3 -> x0, local copies, waits for them, and re-layouts: 8.94 us -> none  [the longest x1 6.8 us: local(): saved = jnp.stack([s[..., 0, :].transpose(4, 1, 3, 0, 2, 5), s[..., 1, :]...]
    another operation x3 -> x0, local copies, waits for them, and re-layouts: 8.89 us -> none  [the longest x1 8.09 us: local(): s = saved_preact[0].reshape(4, 4, 4, 2, 3, 3, 1536)]
    add x4 -> x0, other arithmetic: 6.38 us -> none  [the longest x2 5.75 us: local(): position = block_order[all_rows // 64] * 64 + all_rows % 64]
    gather x10 -> x0, other arithmetic: 6.17 us -> none  [local(): position = block_order[all_rows // 64] * 64 + all_rows % 64]
    slice x2 -> x0, local copies, waits for them, and re-layouts: 4.28 us -> none  [the longest x1 4.26 us: local(): s[..., 0, :].transpose(4, 1, 3, 0, 2, 5)]
    another operation x2 -> x0, other arithmetic: 4.11 us -> none  [the longest x1 4.04 us: local(): jnp.stack([s[..., 0, :].transpose(4, 1, 3, 0, 2, 5), s[..., 1, :].transpo...]
where the time goes in v2:
time: 288 us; the launch traced here: 286 us
  Pallas kernels  278 us (97%)
  local copies, waits for them, and re-layouts  6.76 us (2%)
    pallas_call x1, Pallas kernels, exchange(): pl.pallas_call(exchange_kernel, out_shape=(jax.ShapeDtypeStruct((128, 409...  244 us
    pallas_call x1, Pallas kernels, attention(): pl.pallas_call(attention_kernel, out_shape=(jax.ShapeDtypeStruct((128, 40...  34.5 us
    unnamed x13, local copies, waits for them, and re-layouts  6.76 us

profile of v2, /device:TPU:36, one launch (start us, length us, event | category | flops | bytes accessed | tf_op | source)
XLA Modules:
  0.0 285.9 jit_solution(8416980252121548923)
XLA Ops:
  0.6 0.0 copy-start.4
  0.6 243.9 %shard_map.121 = (bf16[128,4096]{1,0:T(8,128)(2,1)}, bf16[8,128,256]{2,1,0:T(8,128)(2,1)}, bf16[8,128,256]{2,1,0:T(8,128)(2,1)}) custom-call(s32[8,128]{1,0:T(8,128)} %bitcast.32, f32[8,128]{1,0:T(8,128)} %bitcast.33, bf16[128,4096]{1,0:T(8,128)(2,1)} %bitcast.29, bf16[128,256]{1,0:T(8,128)(2,1)} %bitcast.30, bf16[128,256]{1,0:T(8,128)(2,1)} %bitcast.31, ...), custom_call_target="tpu_custom_call" | custom-call | tf_op jit(solution)/shard_map/pallas_call | solution.py:317
  244.5 0.0 copy-done.4
  244.6 0.0 copy-start
  244.6 1.2 copy-done
  245.8 0.0 copy-start.1
  245.8 1.2 copy-done.1
  247.0 0.0 copy-start.2
  247.0 1.0 copy-done.2
  248.0 0.0 copy-start.3
  248.0 1.0 copy-done.3
  249.1 34.5 %shard_map.122 = (bf16[128,4096]{1,0:T(8,128)(2,1)S(1)}, bf16[128,256]{1,0:T(8,128)(2,1)S(1)}, bf16[128,256]{1,0:T(8,128)(2,1)S(1)}) custom-call(s32[16]{0:T(128)S(1)} %copy-done.4, bf16[128,4096]{1,0:T(8,128)(2,1)S(1)} %bitcast.20, bf16[128,4096]{1,0:T(8,128)(2,1)S(1)} %copy-done.1, bf16[1024,256]{1,0:T(8,128)(2,1)S(1)} %bitcast.22, ...), custom_call_target="tpu_custom_call" | custom-call | tf_op jit(solution)/shard_map/pallas_call | solution.py:432
  283.6 1.0 copy.16
  284.6 0.6 copy.17
  285.2 0.6 copy.18
Async XLA Ops:
  0.6 243.9 %copy-start.4 = (s32[16]{0:T(128)S(1)}, s32[16]{0:T(128)}, u32[]{:S(2)}) copy-start(s32[16]{0:T(128)} %order_ref.1) | copy-start | bytes 196
  244.6 1.2 copy-start
  245.8 1.2 copy-start.1
  247.0 1.0 copy-start.2
  248.0 1.0 copy-start.3

commit v3 on v2

--- a/solution.py
+++ b/solution.py
@@ -33,10 +33,11 @@
 
 
 def exchange_kernel(
-    ids_ref, wts_ref, g_ref, k_ref, v_ref, saved_ref, down_ref, gate_ref,
-    res_ref, kf_ref, vf_ref,
+    block_ref, ids_ref, wts_ref, g_ref, q_ref, k_ref, v_ref, saved_ref, down_ref, gate_ref,
+    dq_ref, dk_out, dv_out,
     S, A, B, R, X, act, D, G, sv, acc, rank_ref, mix_ref, order_ref,
-    ssem, rsem, lsem, kvs, kvr, dsem, gsem, svsem,
+    kf_ref, vf_ref, kt, vt, posk_ref, fwd_out, log_total, dk_acc, dv_acc,
+    ssem, rsem, lsem, kvs, kvr, dsem, gsem, svsem, pairs, pairr, outsem,
 ):
     x, y, z, c = coords()
     cc = (x, y, z)
@@ -110,26 +111,44 @@
 
         lax.fori_loop(0, 24, body, 0)
 
-    def combine(j):
-        def body(i, carry):
-            at = j * 12 + i // 2
-            lo = S[at, pl.ds(i % 2 * 2, 2), :, :16, :].reshape(256, 128)
-            hi = S[at, pl.ds(i % 2 * 2, 2), :, 16:, :].reshape(256, 128)
-            unpacked(lo, hi, pl.multiple_of(i * 16, 16))
-            return carry
-
-        lax.fori_loop(0, 24, body, 0)
+    def combine(j, halves=(0, 1)):
+        if len(halves) == 2:
+            def body(i, carry):
+                at = j * 12 + i // 2
+                lo = S[at, pl.ds(i % 2 * 2, 2), :, :16, :].reshape(256, 128)
+                hi = S[at, pl.ds(i % 2 * 2, 2), :, 16:, :].reshape(256, 128)
+                unpacked(lo, hi, pl.multiple_of(i * 16, 16))
+                return carry
+
+            lax.fori_loop(0, 24, body, 0)
+        else:
+            half = halves[0]
+
+            def body(i, carry):
+                at = j * 12 + i
+                x0 = pl.multiple_of(i * 32, 32)
+                lo = S[at, :2, :, half * 16 : half * 16 + 16, :].reshape(256, 128)
+                hi = S[at, 2:, :, half * 16 : half * 16 + 16, :].reshape(256, 128)
+                out = jnp.dot(perm, jnp.concatenate([lo, hi], axis=1), preferred_element_type=F32).astype(BF)
+                for u in range(16):
+                    to = slice(half * 2048 + u * 128, half * 2048 + (u + 1) * 128)
+                    X[pl.ds(x0, 16), to] = out[u * 16 : (u + 1) * 16, :128]
+                    X[pl.ds(x0 + 16, 16), to] = out[u * 16 : (u + 1) * 16, 128:]
+                return carry
+
+            lax.fori_loop(0, 12, body, 0)
         mix = jnp.concatenate(
             [jnp.where(rank_ref[q] == float(3 * j + q), mix_ref[q], 0.0) for q in range(3)], axis=0
         ).T.astype(BF)
-        for h in range(4):
-            cut = slice(h * 1024, (h + 1) * 1024)
-            before = g_ref[:, cut].astype(F32) if j == 0 else acc[:, cut]
-            total = before + jnp.dot(mix, X[:, cut], preferred_element_type=F32)
-            if j < 2:
-                acc[:, cut] = total
-            else:
-                res_ref[:, cut] = total.astype(BF)
+        for half in halves:
+            for h in (2 * half, 2 * half + 1):
+                cut = slice(h * 1024, (h + 1) * 1024)
+                before = g_ref[:, cut].astype(F32) if j == 0 else acc[:, cut]
+                total = before + jnp.dot(mix, X[:, cut], preferred_element_type=F32)
+                if j < 2:
+                    acc[:, cut] = total
+                else:
+                    D[:128, cut] = total.astype(BF)
 
     def saved_copy(j):
         return pltpu.make_async_copy(saved_ref.at[pl.ds(3 * j, 3)], sv, svsem)
@@ -151,7 +170,7 @@
             src, dst, ssem.at[ph, j, q], rsem.at[ph, j, q], device_id=dev, device_id_type=MESH
         )
 
-    def phase(ph, j, q):
+    def phase(ph, j, q, half=None):
         a, b, d = ORDERS[q]
         ma, mb, md = cc[a], cc[b], cc[d]
         n = 3 * j + q
@@ -178,19 +197,25 @@
                         ops.append((B.at[n, :, v * 2 + t], R.at[n, pl.ds((md * 2 + c) * 16, 16)], dv(d, v, t), here))
                     else:
                         ops.append((R.at[n, pl.ds((v * 2 + t) * 16, 16)], B.at[n, :, md * 2 + c], dv(d, v, t), here))
+            at = j + (half or 0)
             for src, dst, dev, here in ops:
+                if half is not None:
+                    cut = (slice(None),) * (len(src.shape) - 2) + (pl.ds(half * 16, 16),)
+                    src, dst = src.at[cut], dst.at[cut]
                 if here:
-                    pltpu.make_async_copy(src, dst, lsem.at[ph, j, q]).start()
+                    pltpu.make_async_copy(src, dst, lsem.at[ph, at, q]).start()
                 else:
-                    remote(src, dst, ph, j, q, dev).start()
-
-    def wait(ph, j, q):
+                    remote(src, dst, ph, at, q, dev).start()
+
+    def wait(ph, j, q, half=None):
         mine = 16 if ph in (2, 3) else 32
-        far = R.at[0, pl.ds(0, 128 - mine)]
-        near = R.at[0, pl.ds(0, mine)]
-        pltpu.make_async_copy(far, far, rsem.at[ph, j, q]).wait()
-        pltpu.make_async_copy(near, near, lsem.at[ph, j, q]).wait()
-        pltpu.make_async_copy(far, far, ssem.at[ph, j, q]).wait()
+        deep = pl.ds(0, 32 if half is None else 16)
+        at = j + (half or 0)
+        far = R.at[0, pl.ds(0, 128 - mine), deep]
+        near = R.at[0, pl.ds(0, mine), deep]
+        pltpu.make_async_copy(far, far, rsem.at[ph, at, q]).wait()
+        pltpu.make_async_copy(near, near, lsem.at[ph, at, q]).wait()
+        pltpu.make_async_copy(far, far, ssem.at[ph, at, q]).wait()
 
     def experts(j):
         def unpack(i, carry):
@@ -253,15 +278,105 @@
 
         lax.fori_loop(0, 24, pack, 0)
 
-    def each(ph, j):
+    def each(ph, j, half=None):
         for q in range(3):
-            phase(ph, j, q)
-
-    def onward(ph, j):
+            phase(ph, j, q, half)
+
+    def onward(ph, j, half=None):
         for q in range(3):
-            wait(ph, j, q)
+            wait(ph, j, q, half)
             if ph not in (2, 5):
-                phase(ph + 1, j, q)
+                phase(ph + 1, j, q, half)
+
+    scale = 1.0 / math.sqrt(HEAD)
+    nt = (((1,), (1,)), ((), ()))
+    within = lax.broadcasted_iota(jnp.int32, (64, 1), 0)
+    for i in range(16):
+        posk_ref[i * 64 : (i + 1) * 64, :] = block_ref[i] * 64 + within
+    token = lax.broadcasted_iota(jnp.int32, (1, 256), 1) & 127
+    posq = jnp.where(token < 64, block_ref[2 * bme] * 64, block_ref[2 * bme + 1] * 64) + (token & 63)
+
+    def two_heads(ref, top, h, i):
+        one = pl.ds(pl.multiple_of((h * 16 + 2 * i) * 128, 128), 128)
+        two = pl.ds(pl.multiple_of((h * 16 + 2 * i + 1) * 128, 128), 128)
+        return jnp.concatenate([ref[top : top + 128, one], ref[top : top + 128, two]], axis=0)
+
+    def scores_of(h, q):
+        keys = kf_ref[:, :, h * 128 : (h + 1) * 128].reshape(1024, 128)
+        scores = lax.dot_general(keys, q, nt, preferred_element_type=F32) * scale
+        return jnp.where(posq >= posk_ref[...], scores, -1e30)
+
+    def attention_forward(h):
+        kt[h] = kf_ref[:, :, h * 128 : (h + 1) * 128].reshape(1024, 128).T
+        vt[h] = vf_ref[:, :, h * 128 : (h + 1) * 128].reshape(1024, 128).T
+
+        def tile(i, carry):
+            scores = scores_of(h, two_heads(q_ref, 0, h, i))
+            top = jnp.max(scores, axis=0, keepdims=True)
+            weights = jnp.exp(scores - top)
+            total = jnp.sum(weights, axis=0, keepdims=True)
+            out = jnp.dot(vt[h], weights.astype(BF), preferred_element_type=F32) / total
+            fwd_out[h * 8 + i] = out.astype(BF)
+            log_total[h * 8 + i] = top + jnp.log(total)
+            return carry
+
+        lax.fori_loop(0, 8, tile, 0)
+
+    def pair_copies(h):
+        rows = pl.ds(256 + 128 * h, 128)
+        for k in range(1, 8):
+            to = (bme + k) & 7
+            yield pltpu.make_async_remote_copy(
+                D.at[rows, pl.ds(pl.multiple_of(to * 256, 256), 256)],
+                D.at[rows, pl.ds(pl.multiple_of(2048 + bme * 256, 256), 256)],
+                pairs.at[h], pairr.at[h], device_id=(to, eme), device_id_type=MESH,
+            )
+
+    def query_copy(h):
+        cols = pl.ds(h * 2048, 2048)
+        return pltpu.make_async_copy(D.at[pl.ds(128, 128), cols], dq_ref.at[:, cols], outsem.at[h])
+
+    def attention_backward(h):
+        dk_acc[...] = jnp.zeros_like(dk_acc)
+        dv_acc[...] = jnp.zeros_like(dv_acc)
+
+        def tile(i, carry):
+            q = two_heads(q_ref, 0, h, i)
+            g = two_heads(D, 0, h, i)
+            delta = jnp.sum(g.astype(F32).T * fwd_out[h * 8 + i].astype(F32), axis=0, keepdims=True)
+            values = vf_ref[:, :, h * 128 : (h + 1) * 128].reshape(1024, 128)
+            prob_grad = lax.dot_general(values, g, nt, preferred_element_type=F32)
+            probs = jnp.exp(scores_of(h, q) - log_total[h * 8 + i])
+            dv_acc[...] += jnp.dot(probs.astype(BF), g, preferred_element_type=F32)
+            score_grad = (probs * (prob_grad - delta)).astype(BF)
+            dk_acc[...] += jnp.dot(score_grad, q, preferred_element_type=F32)
+            dq = (jnp.dot(kt[h], score_grad, preferred_element_type=F32) * scale).T.astype(BF)
+            D[128:256, pl.ds(pl.multiple_of((h * 16 + 2 * i) * 128, 128), 128)] = dq[:128]
+            D[128:256, pl.ds(pl.multiple_of((h * 16 + 2 * i + 1) * 128, 128), 128)] = dq[128:]
+            return carry
+
+        lax.fori_loop(0, 8, tile, 0)
+        query_copy(h).start()
+        rows = slice(256 + 128 * h, 384 + 128 * h)
+        for b in range(8):
+            D[rows, b * 256 : b * 256 + 128] = (dk_acc[b * 128 : (b + 1) * 128, :] * scale).astype(BF)
+            D[rows, b * 256 + 128 : b * 256 + 256] = dv_acc[b * 128 : (b + 1) * 128, :].astype(BF)
+        for copy in pair_copies(h):
+            copy.start()
+        D[rows, pl.ds(pl.multiple_of(2048 + bme * 256, 256), 256)] = D[
+            rows, pl.ds(pl.multiple_of(bme * 256, 256), 256)
+        ]
+
+    def pair_sums(h):
+        rows = slice(256 + 128 * h, 384 + 128 * h)
+        seven = D.at[pl.ds(256 + 128 * h, 128), pl.ds(0, 1792)]
+        pltpu.make_async_copy(seven, seven, pairr.at[h]).wait()
+        pltpu.make_async_copy(seven, seven, pairs.at[h]).wait()
+        total = D[rows, 2048:2304].astype(F32)
+        for b in range(1, 8):
+            total += D[rows, 2048 + b * 256 : 2304 + b * 256].astype(F32)
+        dk_out[:, h * 128 : (h + 1) * 128] = total[:, :128].astype(BF)
+        dv_out[:, h * 128 : (h + 1) * 128] = total[:, 128:].astype(BF)
 
     each(0, 0)
     kf_ref[bme] = k_ref[...]
@@ -276,9 +391,15 @@
     onward(0, 0)
     each(0, 1)
     build(2)
+    for t, full in ((0, kf_ref), (1, vf_ref)):
+        seven = full.at[pl.ds(0, 7)]
+        pltpu.make_async_copy(seven, seven, kvr.at[t]).wait()
+        pltpu.make_async_copy(seven, seven, kvs.at[t]).wait()
+    attention_forward(0)
     onward(1, 0)
     onward(0, 1)
     each(0, 2)
+    attention_forward(1)
     onward(2, 0)
     onward(1, 1)
     onward(0, 2)
@@ -293,24 +414,31 @@
     experts(2)
     onward(4, 0)
     onward(3, 1)
-    each(3, 2)
+    each(3, 2, 0)
+    each(3, 2, 1)
     onward(5, 0)
     combine(0)
     onward(4, 1)
-    onward(3, 2)
-    onward(4, 2)
+    onward(3, 2, 0)
+    onward(3, 2, 1)
     onward(5, 1)
     combine(1)
-    onward(5, 2)
-    combine(2)
-
-    for t, full in ((0, kf_ref), (1, vf_ref)):
-        seven = full.at[pl.ds(0, 7)]
-        pltpu.make_async_copy(seven, seven, kvr.at[t]).wait()
-        pltpu.make_async_copy(seven, seven, kvs.at[t]).wait()
-
-
-def exchange(ids, wts, g, keys, values, saved, down, gate):
+    onward(4, 2, 0)
+    onward(4, 2, 1)
+    onward(5, 2, 0)
+    combine(2, (0,))
+    attention_backward(0)
+    onward(5, 2, 1)
+    combine(2, (1,))
+    attention_backward(1)
+    pair_sums(0)
+    pair_sums(1)
+    query_copy(0).wait()
+    query_copy(1).wait()
+
+
+def exchange(order, ids, wts, g, query, keys, values, saved, down, gate):
+    smem = pl.BlockSpec(memory_space=pltpu.SMEM)
     vmem = pl.BlockSpec(memory_space=pltpu.VMEM)
     hbm = pl.BlockSpec(memory_space=pl.ANY)
     row = (32, 128)
@@ -318,11 +446,11 @@
         exchange_kernel,
         out_shape=(
             jax.ShapeDtypeStruct((128, 4096), BF),
-            jax.ShapeDtypeStruct((8, 128, 256), BF),
-            jax.ShapeDtypeStruct((8, 128, 256), BF),
+            jax.ShapeDtypeStruct((128, 256), BF),
+            jax.ShapeDtypeStruct((128, 256), BF),
         ),
-        in_specs=[vmem] * 5 + [hbm] * 3,
-        out_specs=(vmem, vmem, vmem),
+        in_specs=[smem] + [vmem] * 6 + [hbm] * 3,
+        out_specs=(hbm, vmem, vmem),
         scratch_shapes=[
             pltpu.VMEM((36, 4, 8) + row, BF),
             pltpu.VMEM((9, 4, 4, 8) + row, BF),
@@ -337,136 +465,46 @@
             pltpu.VMEM((3, 128, 128), F32),
             pltpu.VMEM((3, 128, 128), F32),
             pltpu.VMEM((3, 128, 128), BF),
-            pltpu.SemaphoreType.DMA((6, 3, 3)),
-            pltpu.SemaphoreType.DMA((6, 3, 3)),
-            pltpu.SemaphoreType.DMA((6, 3, 3)),
+            pltpu.VMEM((8, 128, 256), BF),
+            pltpu.VMEM((8, 128, 256), BF),
+            pltpu.VMEM((2, 128, 1024), BF),
+            pltpu.VMEM((2, 128, 1024), BF),
+            pltpu.VMEM((1024, 1), jnp.int32),
+            pltpu.VMEM((16, 128, 256), BF),
+            pltpu.VMEM((16, 1, 256), F32),
+            pltpu.VMEM((1024, 128), F32),
+            pltpu.VMEM((1024, 128), F32),
+            pltpu.SemaphoreType.DMA((6, 4, 3)),
+            pltpu.SemaphoreType.DMA((6, 4, 3)),
+            pltpu.SemaphoreType.DMA((6, 4, 3)),
             pltpu.SemaphoreType.DMA((2,)),
             pltpu.SemaphoreType.DMA((2,)),
             pltpu.SemaphoreType.DMA,
             pltpu.SemaphoreType.DMA((2,)),
             pltpu.SemaphoreType.DMA,
+            pltpu.SemaphoreType.DMA((2,)),
+            pltpu.SemaphoreType.DMA((2,)),
+            pltpu.SemaphoreType.DMA((2,)),
         ],
         compiler_params=pltpu.CompilerParams(
             collective_id=0, has_side_effects=True, vmem_limit_bytes=63 << 20
         ),
-    )(ids, wts, g, keys, values, saved, down, gate)
-
-
-def attention_kernel(
-    order_ref, q_ref, res_ref, k_ref, v_ref,
-    dq_ref, dk_out, dv_out,
-    posk_ref, kt, vt, dk_acc, dv_acc, part, got, ssem, rsem,
-):
-    bme = lax.axis_index("blk")
-    eme = lax.axis_index("expert")
-    barrier = pltpu.get_barrier_semaphore()
-    for k in range(1, 8):
-        pl.semaphore_signal(barrier, inc=1, device_id=((bme + k) & 7, eme), device_id_type=MESH)
-    scale = 1.0 / math.sqrt(HEAD)
-    within = lax.broadcasted_iota(jnp.int32, (64, 1), 0)
-    for i in range(16):
-        posk_ref[i * 64 : (i + 1) * 64, :] = order_ref[i] * 64 + within
-    lanes = lax.broadcasted_iota(jnp.int32, (1, 256), 1) & 127
-    posq = jnp.where(lanes < 64, order_ref[2 * bme] * 64, order_ref[2 * bme + 1] * 64) + (lanes & 63)
-
-    def copies(h):
-        for k in range(1, 8):
-            to = (bme + k) & 7
-            yield pltpu.make_async_remote_copy(
-                part.at[h, to], got.at[h, bme], ssem.at[h], rsem.at[h], device_id=(to, eme), device_id_type=MESH
-            )
-
-    for h in range(2):
-        keys = k_ref[:, h * 128 : (h + 1) * 128]
-        values = v_ref[:, h * 128 : (h + 1) * 128]
-        kt[...] = keys.T
-        vt[...] = values.T
-        dk_acc[...] = jnp.zeros_like(dk_acc)
-        dv_acc[...] = jnp.zeros_like(dv_acc)
-
-        def tile(i, carry):
-            one = pl.ds(pl.multiple_of((h * 16 + 2 * i) * 128, 128), 128)
-            two = pl.ds(pl.multiple_of((h * 16 + 2 * i + 1) * 128, 128), 128)
-            q = jnp.concatenate([q_ref[:, one], q_ref[:, two]], axis=0)
-            g = jnp.concatenate([res_ref[:, one], res_ref[:, two]], axis=0)
-            nt = (((1,), (1,)), ((), ()))
-            scores = lax.dot_general(k_ref[:, h * 128 : (h + 1) * 128], q, nt, preferred_element_type=F32) * scale
-            scores = jnp.where(posq >= posk_ref[...], scores, -1e30)
-            top = jnp.max(scores, axis=0, keepdims=True)
-            weights = jnp.exp(scores - top)
-            inverse = 1.0 / jnp.sum(weights, axis=0, keepdims=True)
-            out = jnp.dot(vt[...], weights.astype(BF), preferred_element_type=F32) * inverse
-            delta = jnp.sum(g.astype(F32).T * out, axis=0, keepdims=True)
-            probs = weights * inverse
-            dv_acc[...] += jnp.dot(probs.astype(BF), g, preferred_element_type=F32)
-            prob_grad = lax.dot_general(v_ref[:, h * 128 : (h + 1) * 128], g, nt, preferred_element_type=F32)
-            score_grad = (probs * (prob_grad - delta)).astype(BF)
-            dk_acc[...] += jnp.dot(score_grad, q, preferred_element_type=F32)
-            dq = (jnp.dot(kt[...], score_grad, preferred_element_type=F32) * scale).T.astype(BF)
-            dq_ref[:, one] = dq[:128]
-            dq_ref[:, two] = dq[128:]
-            return carry
-
-        lax.fori_loop(0, 8, tile, 0)
-        part[h, :, 0] = (dk_acc[...] * scale).astype(BF).reshape(8, 128, 128)
-        part[h, :, 1] = dv_acc[...].astype(BF).reshape(8, 128, 128)
-        got[h, bme] = part[h, bme]
-        if h == 0:
-            pl.semaphore_wait(barrier, 7)
-        for copy in copies(h):
-            copy.start()
-
-    for h in range(2):
-        seven = got.at[h, pl.ds(0, 7)]
-        pltpu.make_async_copy(seven, seven, rsem.at[h]).wait()
-        pltpu.make_async_copy(seven, seven, ssem.at[h]).wait()
-        for t, out in ((0, dk_out), (1, dv_out)):
-            total = got[h, 0, t].astype(F32)
-            for s in range(1, 8):
-                total += got[h, s, t].astype(F32)
-            out[:, h * 128 : (h + 1) * 128] = total.astype(BF)
-
-
-def attention(order, query, res, keys, values):
-    vmem = pl.BlockSpec(memory_space=pltpu.VMEM)
-    return pl.pallas_call(
-        attention_kernel,
-        out_shape=(
-            jax.ShapeDtypeStruct((128, 4096), BF),
-            jax.ShapeDtypeStruct((128, 256), BF),
-            jax.ShapeDtypeStruct((128, 256), BF),
-        ),
-        in_specs=[pl.BlockSpec(memory_space=pltpu.SMEM)] + [vmem] * 4,
-        out_specs=(vmem,) * 3,
-        scratch_shapes=[
-            pltpu.VMEM((1024, 1), jnp.int32),
-            pltpu.VMEM((128, 1024), BF),
-            pltpu.VMEM((128, 1024), BF),
-            pltpu.VMEM((1024, 128), F32),
-            pltpu.VMEM((1024, 128), F32),
-            pltpu.VMEM((2, 8, 2, 128, 128), BF),
-            pltpu.VMEM((2, 8, 2, 128, 128), BF),
-            pltpu.SemaphoreType.DMA((2,)),
-            pltpu.SemaphoreType.DMA((2,)),
-        ],
-        compiler_params=pltpu.CompilerParams(
-            collective_id=1, has_side_effects=True, vmem_limit_bytes=40 << 20
-        ),
-    )(order, query, res, keys, values)
+    )(order, ids, wts, g, query, keys, values, saved, down, gate)
 
 
 def local(query, keys, values, grad_output, expert_ids, gate_weights, gate_up, down_weight, saved_preact, block_order):
-    res, kf, vf = exchange(
+    dq, dk, dv = exchange(
+        block_order,
         expert_ids[0].T,
         gate_weights[0].T,
         grad_output[0],
+        query[0],
         keys[0],
         values[0],
         saved_preact[0].transpose(1, 0, 2),
         down_weight[0],
         gate_up[0],
     )
-    dq, dk, dv = attention(block_order, query[0], res, kf.reshape(1024, 256), vf.reshape(1024, 256))
     return dq[None], dk[None], dv[None]
 
 

time: 288 us -> 272 us (0.944)
  Pallas kernels: 278 us -> 262 us
    pallas_call x1 -> x0, Pallas kernels: 34.5 us -> none  [attention(): pl.pallas_call(attention_kernel, out_shape=(jax.ShapeDtypeStruct((128, 40...]
    pallas_call x1, Pallas kernels: 244 us -> 262 us  [exchange(): pl.pallas_call(exchange_kernel, out_shape=(jax.ShapeDtypeStruct((128, 409...]
    unnamed x13 -> x3, local copies, waits for them, and re-layouts: 6.76 us -> 5.23 us
where the time goes in v3:
time: 272 us; the launch traced here: 268 us
  Pallas kernels  262 us (96%)
  local copies, waits for them, and re-layouts  5.23 us (2%)
    pallas_call x1, Pallas kernels, exchange(): pl.pallas_call(exchange_kernel, out_shape=(jax.ShapeDtypeStruct((128, 409...  262 us

profile of v3, /device:TPU:36, one launch (start us, length us, event | category | flops | bytes accessed | tf_op | source)
XLA Modules:
  0.0 267.8 jit_solution(3725192697332642512)
XLA Ops:
  0.6 261.9 %shard_map.121 = (bf16[128,4096]{1,0:T(8,128)(2,1)}, bf16[128,256]{1,0:T(8,128)(2,1)}, bf16[128,256]{1,0:T(8,128)(2,1)}) custom-call(s32[16]{0:T(128)} %block_ref.1, s32[8,128]{1,0:T(8,128)} %bitcast.28, f32[8,128]{1,0:T(8,128)} %bitcast.29, bf16[128,4096]{1,0:T(8,128)(2,1)} %bitcast.21, bf16[128,4096]{1,0:T(8,128)(2,1)} %bitcast.22, ...), custom_call_target="tpu_custom_call" | custom-call | tf_op jit(solution)/shard_map/pallas_call | solution.py:445
  262.5 2.3 copy.16
  264.8 1.5 copy.17
  266.3 1.5 copy.18

commit v4 on v3

--- a/solution.py
+++ b/solution.py
@@ -94,22 +94,21 @@
         hi = jnp.concatenate([X[pl.ds(x0, 16), 2048 + u * 128 : 2048 + (u + 1) * 128] for u in range(16)], axis=0)
         return jnp.dot(perm, jnp.concatenate([lo, hi], axis=1), preferred_element_type=F32).astype(BF)
 
-    def build(j):
-        for q in range(3):
-            pick = jnp.where(rank_ref[q] == float(3 * j + q), 1.0, 0.0).astype(BF)
-            for h in range(4):
-                X[q * 128 : (q + 1) * 128, h * 1024 : (h + 1) * 1024] = jnp.dot(
-                    pick, g_ref[:, h * 1024 : (h + 1) * 1024], preferred_element_type=F32
-                ).astype(BF)
+    def build(j, q):
+        pick = jnp.where(rank_ref[q] == float(3 * j + q), 1.0, 0.0).astype(BF)
+        for h in range(4):
+            X[q * 128 : (q + 1) * 128, h * 1024 : (h + 1) * 1024] = jnp.dot(
+                pick, g_ref[:, h * 1024 : (h + 1) * 1024], preferred_element_type=F32
+            ).astype(BF)
 
         def body(i, carry):
-            out = packed(pl.multiple_of(i * 16, 16))
-            at = j * 12 + i // 2
+            out = packed(pl.multiple_of(q * 128 + i * 16, 16))
+            at = (j * 3 + q) * 4 + i // 2
             S[at, pl.ds(i % 2 * 2, 2), :, :16, :] = out[:, :128].reshape(2, 8, 16, 128)
             S[at, pl.ds(i % 2 * 2, 2), :, 16:, :] = out[:, 128:].reshape(2, 8, 16, 128)
             return carry
 
-        lax.fori_loop(0, 24, body, 0)
+        lax.fori_loop(0, 8, body, 0)
 
     def combine(j, halves=(0, 1)):
         if len(halves) == 2:
@@ -162,7 +161,7 @@
         source = t[1] * 32 + t[2] * 8 + t[0] * 2 + ((sub >> 4) & 1)
         order_ref[q] = jnp.where(lane == source, 1.0, 0.0).astype(BF)
 
-    build(0)
+    build(0, 0)
     pl.semaphore_wait(barrier, len(peers))
 
     def remote(src, dst, ph, j, q, dev):
@@ -320,7 +319,7 @@
             log_total[h * 8 + i] = top + jnp.log(total)
             return carry
 
-        lax.fori_loop(0, 8, tile, 0)
+        lax.fori_loop(0, 8, tile, 0, unroll=2)
 
     def pair_copies(h):
         rows = pl.ds(256 + 128 * h, 128)
@@ -355,7 +354,7 @@
             D[128:256, pl.ds(pl.multiple_of((h * 16 + 2 * i + 1) * 128, 128), 128)] = dq[128:]
             return carry
 
-        lax.fori_loop(0, 8, tile, 0)
+        lax.fori_loop(0, 8, tile, 0, unroll=2)
         query_copy(h).start()
         rows = slice(256 + 128 * h, 384 + 128 * h)
         for b in range(8):
@@ -378,7 +377,10 @@
         dk_out[:, h * 128 : (h + 1) * 128] = total[:, :128].astype(BF)
         dv_out[:, h * 128 : (h + 1) * 128] = total[:, 128:].astype(BF)
 
-    each(0, 0)
+    phase(0, 0, 0)
+    for q in (1, 2):
+        build(0, q)
+        phase(0, 0, q)
     kf_ref[bme] = k_ref[...]
     vf_ref[bme] = v_ref[...]
     for k in range(1, 8):
@@ -387,22 +389,24 @@
             pltpu.make_async_remote_copy(
                 src, dst.at[bme], kvs.at[t], kvr.at[t], device_id=(to, eme), device_id_type=MESH
             ).start()
-    build(1)
-    onward(0, 0)
-    each(0, 1)
-    build(2)
+    for q in range(3):
+        build(1, q)
+        phase(0, 1, q)
+    for q in range(3):
+        build(2, q)
     for t, full in ((0, kf_ref), (1, vf_ref)):
         seven = full.at[pl.ds(0, 7)]
         pltpu.make_async_copy(seven, seven, kvr.at[t]).wait()
         pltpu.make_async_copy(seven, seven, kvs.at[t]).wait()
+    onward(0, 0)
+    each(0, 2)
     attention_forward(0)
+    onward(0, 1)
     onward(1, 0)
-    onward(0, 1)
-    each(0, 2)
     attention_forward(1)
+    onward(0, 2)
     onward(2, 0)
     onward(1, 1)
-    onward(0, 2)
     experts(0)
     onward(2, 1)
     onward(1, 2)
@@ -416,14 +420,14 @@
     onward(3, 1)
     each(3, 2, 0)
     each(3, 2, 1)
+    onward(4, 1)
+    onward(3, 2, 0)
     onward(5, 0)
     combine(0)
-    onward(4, 1)
-    onward(3, 2, 0)
     onward(3, 2, 1)
+    onward(4, 2, 0)
     onward(5, 1)
     combine(1)
-    onward(4, 2, 0)
     onward(4, 2, 1)
     onward(5, 2, 0)
     combine(2, (0,))
@@ -492,6 +496,27 @@
     )(order, ids, wts, g, query, keys, values, saved, down, gate)
 
 
+def handed_over_kernel(a_ref, b_ref, c_ref, a_out, b_out, c_out, sem):
+    pairs = ((a_ref, a_out), (b_ref, b_out), (c_ref, c_out))
+    copies = [pltpu.make_async_copy(src, dst, sem.at[i]) for i, (src, dst) in enumerate(pairs)]
+    for copy in copies:
+        copy.start()
+    for copy in copies:
+        copy.wait()
+
+
+def handed_over(*arrays):
+    hbm = pl.BlockSpec(memory_space=pl.ANY)
+    return pl.pallas_call(
+        handed_over_kernel,
+        out_shape=tuple(jax.ShapeDtypeStruct(a.shape, a.dtype) for a in arrays),
+        in_specs=[hbm] * 3,
+        out_specs=(hbm,) * 3,
+        scratch_shapes=[pltpu.SemaphoreType.DMA((3,))],
+        compiler_params=pltpu.CompilerParams(vmem_limit_bytes=63 << 20),
+    )(*arrays)
+
+
 def local(query, keys, values, grad_output, expert_ids, gate_weights, gate_up, down_weight, saved_preact, block_order):
     dq, dk, dv = exchange(
         block_order,
@@ -505,6 +530,7 @@
         down_weight[0],
         gate_up[0],
     )
+    dq, dk, dv = handed_over(dq, dk, dv)
     return dq[None], dk[None], dv[None]
 
 

time: 272 us -> 304 us (1.12)
  Pallas kernels: 262 us -> 300 us
  local copies, waits for them, and re-layouts: 5.23 us -> 0 us
    pallas_call x0 -> x1, Pallas kernels: none -> 36.9 us  [handed_over(): pl.pallas_call(handed_over_kernel, out_shape=tuple((jax.ShapeDtypeStruct(...]
    unnamed x3 -> x0, local copies, waits for them, and re-layouts: 5.23 us -> none
where the time goes in v4:
time: 304 us; the launch traced here: 301 us
  Pallas kernels  300 us (99%)
    pallas_call x1, Pallas kernels, exchange(): pl.pallas_call(exchange_kernel, out_shape=(jax.ShapeDtypeStruct((128, 409...  263 us
    pallas_call x1, Pallas kernels, handed_over(): pl.pallas_call(handed_over_kernel, out_shape=tuple((jax.ShapeDtypeStruct(...  36.9 us

profile of v4, /device:TPU:36, one launch (start us, length us, event | category | flops | bytes accessed | tf_op | source)
XLA Modules:
  0.0 301.0 jit_solution(1810607509767081831)
XLA Ops:
  0.6 263.3 %shard_map.121 = (bf16[128,4096]{1,0:T(8,128)(2,1)}, bf16[128,256]{1,0:T(8,128)(2,1)}, bf16[128,256]{1,0:T(8,128)(2,1)}) custom-call(s32[16]{0:T(128)} %block_ref.1, s32[8,128]{1,0:T(8,128)} %bitcast.25, f32[8,128]{1,0:T(8,128)} %bitcast.26, bf16[128,4096]{1,0:T(8,128)(2,1)} %bitcast.21, bf16[128,4096]{1,0:T(8,128)(2,1)} %bitcast.22, ...), custom_call_target="tpu_custom_call" | custom-call | tf_op jit(solution)/shard_map/pallas_call | solution.py:449
  264.0 36.9 %shard_map.122 = (bf16[128,4096]{1,0:T(8,128)(2,1)}, bf16[128,256]{1,0:T(8,128)(2,1)}, bf16[128,256]{1,0:T(8,128)(2,1)}) custom-call(bf16[128,4096]{1,0:T(8,128)(2,1)} %get-tuple-element.9.a_ref, bf16[128,256]{1,0:T(8,128)(2,1)} %get-tuple-element.10.b_ref, bf16[128,256]{1,0:T(8,128)(2,1)} %get-tuple-element.11.c_ref), custom_call_target="tpu_custom_call" | custom-call | tf_op jit(solution)/shard_map/pallas_call | solution.py:510

commit v5 on v3

--- a/solution.py
+++ b/solution.py
@@ -492,6 +492,24 @@
     )(order, ids, wts, g, query, keys, values, saved, down, gate)
 
 
+def handed_over_kernel(a_ref, b_ref, c_ref, a_out, b_out, c_out):
+    a_out[...] = a_ref[...]
+    b_out[...] = b_ref[...]
+    c_out[...] = c_ref[...]
+
+
+def handed_over(*arrays):
+    specs = [pl.BlockSpec((64, a.shape[1]), lambda i: (i, 0)) for a in arrays]
+    return pl.pallas_call(
+        handed_over_kernel,
+        grid=(2,),
+        out_shape=tuple(jax.ShapeDtypeStruct(a.shape, a.dtype) for a in arrays),
+        in_specs=specs,
+        out_specs=specs,
+        compiler_params=pltpu.CompilerParams(vmem_limit_bytes=63 << 20),
+    )(*arrays)
+
+
 def local(query, keys, values, grad_output, expert_ids, gate_weights, gate_up, down_weight, saved_preact, block_order):
     dq, dk, dv = exchange(
         block_order,
@@ -505,6 +523,7 @@
         down_weight[0],
         gate_up[0],
     )
+    dq, dk, dv = handed_over(dq, dk, dv)
     return dq[None], dk[None], dv[None]
 
 

time: 272 us -> 269 us (0.989)
  local copies, waits for them, and re-layouts: 5.23 us -> 0 us
    unnamed x3 -> x0, local copies, waits for them, and re-layouts: 5.23 us -> none
where the time goes in v5:
time: 269 us; the launch traced here: 265 us
  Pallas kernels  264 us (98%)
    pallas_call x1, Pallas kernels, exchange(): pl.pallas_call(exchange_kernel, out_shape=(jax.ShapeDtypeStruct((128, 409...  262 us

profile of v5, /device:TPU:36, one launch (start us, length us, event | category | flops | bytes accessed | tf_op | source)
XLA Modules:
  0.0 264.6 jit_solution(12457858746383884955)
XLA Ops:
  0.6 261.9 %shard_map.121 = (bf16[128,4096]{1,0:T(8,128)(2,1)}, bf16[128,256]{1,0:T(8,128)(2,1)}, bf16[128,256]{1,0:T(8,128)(2,1)}) custom-call(s32[16]{0:T(128)} %block_ref.1, s32[8,128]{1,0:T(8,128)} %bitcast.25, f32[8,128]{1,0:T(8,128)} %bitcast.26, bf16[128,4096]{1,0:T(8,128)(2,1)} %bitcast.21, bf16[128,4096]{1,0:T(8,128)(2,1)} %bitcast.22, ...), custom_call_target="tpu_custom_call" | custom-call | tf_op jit(solution)/shard_map/pallas_call | solution.py:445
  262.5 2.1 shard_map.122
